TPU v7x, 32 devices: a whole 2x2x4 slice. The times are simulated.
32 devices in a mesh: groups: 2 (over y), wide: 4 (over z), slab: 2 (over x), sub: 2 (over core).
Axes of the slice: x: 2, y: 2, z: 4, core: 2. Of those that a mesh axis runs over, the one named last changes fastest.
Arguments:
- source: bfloat16 [16, 64, 2, 32, 128], P(('groups', 'slab'), 'wide', None, 'sub'), parts along dimension 0, may hold values from -6 to 6
- aggregation: bfloat16 [2, 1024, 128], P(None, 'groups'), parts along dimension 1, may hold values from -0.375 to 0.375
- translators: bfloat16 [2, 1024, 31, 255], P(None, ('groups', 'wide')), parts along dimension 1, may hold values from -0.1875 to 0.1875
- tile_map: int32 [8, 8], replicated, may hold values from 0 to 30, as said below
- far_mask: int32 [8, 8], replicated, may hold values from 0 to 1
- box_offsets: int32 [64, 64], replicated, may hold values from 0 to 254, as said below
- disaggregation: bfloat16 [2, 128, 1024], P(None, None, 'groups'), parts along dimension 2, may hold values from -0.1875 to 0.1875
Outputs:
- field: bfloat16 [16, 64, 2, 32, 128], P(('groups', 'slab'), 'wide', None, 'sub'), parts along dimension 0
There are 2 independent parts, one for each index of `groups`. A program takes and returns all parts, laid end to end along the dimension named above; an argument that names none is the same for every part. Nothing has to cross between parts.
Inputs may be any that keep to these rules, and one draw needn't show every extreme that they name: tile_map[a, c] = row[a] - row[c] + 16 - 1, where row holds the distinct grid rows of the rows of boxes in increasing order, row[0] = 0 and row[last] = 16 - 1; far_mask[a, c] = 1 exactly where |row[a] - row[c]| >= 2. `box_offsets`: offset index of a pair of boxes of one row.
All inputs are finite; a program needn't handle non-finite values.
Results may differ from a plain program's by a relative error of at most 0.0058.
Values may be sent and summed in bfloat16 or wider, within the bound.
No kernel may reach another device: no remote copies, remote signals or barrier semaphores. Data moves between devices by JAX's collectives and lax.ppermute only.
A program may use at most 192 MiB of HBM per device.

v0:
```python
import functools

import jax
import jax.numpy as jnp
from jax import lax
from jax.experimental import pallas as pl
from jax.experimental.pallas import tpu as pltpu
from jax.sharding import PartitionSpec as P

OWNERS = ("wide", "slab", "sub")
LANES = 128
VMEM = 56 * 1024 * 1024
PITCH = 36
NT = (((1,), (1,)), ((), ()))
TN = (((0,), (0,)), ((), ()))


def outgoing_kernel(boxes, illum, devices, half, src_ref, agg_ref, out_ref, wide_src, wide_out):
    unknowns = src_ref.shape[1]
    wide_src[...] = src_ref[...].astype(jnp.float32)
    real = agg_ref[0].astype(jnp.float32)
    imag = agg_ref[1].astype(jnp.float32)

    def pick(array, part):
        return jnp.concatenate(
            [array[(2 * d + part) * half:(2 * d + part + 1) * half] for d in range(devices)], axis=0
        )

    real_low, real_high = pick(real, 0), pick(real, 1)
    imag_low, imag_high = pick(imag, 0), pick(imag, 1)
    to_real = jnp.concatenate([real_low, -imag_low, real_high, -imag_high], axis=1).astype(jnp.bfloat16)
    to_imag = jnp.concatenate([imag_low, real_low, imag_high, real_high], axis=1).astype(jnp.bfloat16)
    zeros = jnp.zeros((boxes, 2 * unknowns), jnp.bfloat16)
    rows = devices * half
    for r in range(illum):
        both = jnp.concatenate(
            [wide_src[pl.ds(q * illum + r, boxes, stride=2 * illum), :] for q in range(2)], axis=1
        ).astype(jnp.bfloat16)
        right = jnp.concatenate(
            [jnp.concatenate([both, zeros], axis=1), jnp.concatenate([zeros, both], axis=1)], axis=0
        )
        for q, left in ((0, to_real), (1, to_imag)):
            wide_out[pl.ds(q * illum + r, rows, stride=PITCH), :] = lax.dot_general(
                left, right, NT, preferred_element_type=jnp.float32
            )
    tall = 2 * illum
    for g in range(rows):
        out_ref[g * tall:(g + 1) * tall] = wide_out[g * PITCH:g * PITCH + tall].astype(jnp.bfloat16)


def expand_kernel(middle, base_ref, index_ref, table_ref, out_ref, choice, left, wide):
    batch, translators, offsets = table_ref.shape[1:]
    depth = out_ref.shape[3]
    tall = 2 * depth
    rows = 2 * batch * tall

    @pl.when(pl.program_id(0) == 0)
    def _():
        offset = lax.broadcasted_iota(jnp.int32, (2 * LANES, LANES), 0)
        for x in range(tall):
            choice[:, x * LANES:(x + 1) * LANES] = jnp.where(
                offset == index_ref[x:x + 1, :], 1.0, 0.0
            ).astype(jnp.bfloat16)
        left[...] = jnp.zeros_like(left)

    for q in range(2):
        for k in range(batch):
            row = (q * batch + k) * tall
            left[row:row + translators, 0:offsets] = table_ref[q, k]
    table = left[...]
    for x in range(0, tall, 2):
        picked = jnp.dot(
            table, choice[:, x * LANES:(x + 2) * LANES], preferred_element_type=jnp.float32
        )
        wide[pl.ds(x, rows, stride=PITCH), :] = picked[:, :LANES]
        wide[pl.ds(x + 1, rows, stride=PITCH), :] = picked[:, LANES:]
    for k in range(batch):
        for v in range(2):
            out_ref[v, k, middle] = jnp.zeros(out_ref.shape[3:], jnp.bfloat16)
        for t in range(translators):
            if abs(t - middle) < 2:
                continue
            for q in range(2):
                row = ((q * batch + k) * tall + t) * PITCH
                for v in range(2):
                    out_ref[v, k, t, :, q * LANES:(q + 1) * LANES] = wide[
                        row + v * depth:row + (v + 1) * depth
                    ].astype(jnp.bfloat16)


def translate_kernel(wide, slab, sub, rows, columns, pair_ref, src_ref, exp_ref, out_ref):
    illum = src_ref.shape[3]
    steps = exp_ref.shape[2]
    all_rows = slab * rows
    lane = lax.broadcasted_iota(jnp.int32, (illum, LANES), 1)
    group = lane // columns
    groups = LANES // columns
    lower = lane < LANES // 2
    zero = jnp.zeros((illum, LANES), jnp.bfloat16)
    for step in range(steps):
        here = pl.program_id(0) * steps + step
        sums = [None, None]
        turned = {}

        def turn(s, u, q, w, amount):
            key = (s, u, q, w, amount)
            if key not in turned:
                tile = src_ref[(w * slab + s) * sub + u, here, q]
                turned[key] = pltpu.roll(tile, amount * columns, 1) if amount else tile
            return turned[key]

        for c in range(all_rows):
            s, own = c // rows, c % rows
            for k2 in range(2):
                position = k2 * rows + own
                parts = {}
                for u in range(sub):
                    for q in range(2):
                        for h in range(2):
                            tile = zero
                            for w in range(wide):
                                place = h * wide + w
                                tile = jnp.where(
                                    group == place,
                                    turn(s, u, q, w, (place - position) % groups),
                                    tile,
                                )
                            parts[u, q, h] = tile
                left = []
                for h in range(2):
                    for u in range(sub):
                        left.append(jnp.concatenate([parts[u, 0, h], -parts[u, 1, h]], axis=1))
                        left.append(jnp.concatenate([parts[u, 1, h], parts[u, 0, h]], axis=1))
                left = jnp.concatenate(left, axis=0)
                right = jnp.concatenate(
                    [exp_ref[0, k2, step, pair_ref[a * all_rows + c]] for a in range(all_rows)], axis=0
                )
                product = lax.dot_general(left, right, NT, preferred_element_type=jnp.float32)
                sums[k2] = product if sums[k2] is None else sums[k2] + product
        for h in range(2):
            for u in range(sub):
                for q in range(2):
                    row = ((h * sub + u) * 2 + q) * illum
                    first = sums[0][row:row + illum]
                    second = sums[1][row:row + illum]
                    for s in range(slab):
                        if s == 0:
                            tile = jnp.where(lower, first, pltpu.roll(second, LANES // 2, 1))
                        else:
                            tile = jnp.where(lower, pltpu.roll(first, LANES // 2, 1), second)
                        out_ref[(h * slab + s) * sub + u, here, q] = tile.astype(jnp.bfloat16)


def pattern_kernel(devices, half, place_ref, dis_ref, out_ref):
    real = dis_ref[0].astype(jnp.float32).T
    imag = dis_ref[1].astype(jnp.float32).T

    def pick(array, part):
        return jnp.concatenate(
            [array[(2 * d + part) * half:(2 * d + part + 1) * half] for d in range(devices)], axis=0
        )

    sides = []
    for part in range(2):
        real_part, imag_part = pick(real, part), pick(imag, part)
        sides.append(
            jnp.concatenate(
                [
                    jnp.concatenate([real_part, imag_part], axis=1),
                    jnp.concatenate([-imag_part, real_part], axis=1),
                ],
                axis=0,
            )
        )
    out_ref[...] = jnp.concatenate(sides, axis=1).astype(jnp.bfloat16)


def field_kernel(boxes, illum, inc_ref, pattern_ref, out_ref, wide_inc, wide_out):
    unknowns = out_ref.shape[1]
    tall = 2 * illum
    rows = inc_ref.shape[0] // tall
    for g in range(rows):
        wide_inc[g * PITCH:g * PITCH + tall] = inc_ref[g * tall:(g + 1) * tall].astype(jnp.float32)
    right = pattern_ref[...]
    for r in range(illum):
        left = jnp.concatenate(
            [wide_inc[pl.ds(q * illum + r, rows, stride=PITCH), :] for q in range(2)], axis=0
        ).astype(jnp.bfloat16)
        product = lax.dot_general(left, right, TN, preferred_element_type=jnp.float32)
        total = product[:boxes, :2 * unknowns] + product[boxes:, 2 * unknowns:]
        for q in range(2):
            wide_out[pl.ds(q * illum + r, boxes, stride=PITCH), :] = total[
                :, q * unknowns:(q + 1) * unknowns
            ]
    for g in range(boxes):
        out_ref[g * tall:(g + 1) * tall] = wide_out[g * PITCH:g * PITCH + tall].astype(out_ref.dtype)


def tiled_local(wide, slab, sub, source, aggregation, translators, tile_map, far_mask, box_offsets, disaggregation):
    rows, columns, _, illum, unknowns = source.shape
    devices = wide * slab * sub
    directions = aggregation.shape[1]
    half = directions // devices // 2
    boxes = rows * columns
    all_rows = slab * rows
    count = translators.shape[2]
    offsets = translators.shape[3]
    middle = count // 2
    params = pltpu.CompilerParams(vmem_limit_bytes=VMEM)

    lines = devices * half * 2 * illum
    outgoing = pl.pallas_call(
        functools.partial(outgoing_kernel, boxes, illum, devices, half),
        out_shape=jax.ShapeDtypeStruct((lines, LANES), jnp.bfloat16),
        scratch_shapes=[
            pltpu.VMEM((boxes * 2 * illum, unknowns), jnp.float32),
            pltpu.VMEM((devices * half * PITCH, LANES), jnp.float32),
        ],
        compiler_params=params,
        name="outgoing",
    )(source.reshape(boxes * 2 * illum, unknowns), aggregation)
    block = (devices, half, 2, illum, LANES)
    received = lax.all_to_all(outgoing.reshape(block), OWNERS, split_axis=0, concat_axis=0, tiled=True)

    side = box_offsets.shape[0]
    x_half = side // 2
    place = lax.axis_index("wide") // 2
    by_side = jnp.where(place == 0, jnp.roll(box_offsets, x_half, axis=0), box_offsets)
    by_side = by_side.reshape(2, 2, columns, side)
    index = jnp.concatenate([by_side[:, 0], by_side[:, 1]], axis=-1).reshape(x_half, 2 * side)
    base = lax.axis_index("slab") * sub + lax.axis_index("sub")
    near = devices // 2
    pattern = pl.pallas_call(
        functools.partial(pattern_kernel, near, half),
        grid_spec=pltpu.PrefetchScalarGridSpec(
            num_scalar_prefetch=1,
            grid=(1,),
            in_specs=[pl.BlockSpec((2, unknowns, directions // 2), lambda i, place: (0, 0, place[0]))],
            out_specs=pl.BlockSpec((2 * near * half, 4 * unknowns), lambda i, place: (0, 0)),
        ),
        out_shape=jax.ShapeDtypeStruct((2 * near * half, 4 * unknowns), jnp.bfloat16),
        compiler_params=params,
        name="pattern",
    )(place.reshape(1), disaggregation)
    index, pattern = lax.optimization_barrier((index, pattern))
    batch = 4
    expanded = pl.pallas_call(
        functools.partial(expand_kernel, middle),
        grid_spec=pltpu.PrefetchScalarGridSpec(
            num_scalar_prefetch=1,
            grid=(2 * half // batch,),
            in_specs=[
                pl.BlockSpec((x_half, 2 * side), lambda k, base: (0, 0)),
                pl.BlockSpec(
                    (2, batch, count, offsets), lambda k, base: (0, base[0] * (2 * half // batch) + k, 0, 0)
                ),
            ],
            out_specs=pl.BlockSpec(
                (2, batch, count, columns, 2 * LANES), lambda k, base: (0, k, 0, 0, 0)
            ),
            scratch_shapes=[
                pltpu.VMEM((2 * LANES, x_half * LANES), jnp.bfloat16),
                pltpu.VMEM((2 * batch * x_half, 2 * LANES), jnp.bfloat16),
                pltpu.VMEM((2 * batch * x_half * PITCH, LANES), jnp.float32),
            ],
        ),
        out_shape=jax.ShapeDtypeStruct((2, 2 * half, count, columns, 2 * LANES), jnp.bfloat16),
        compiler_params=params,
        name="expand",
    )(base.reshape(1), index, translators)
    expanded = expanded.reshape(2, 2, half, count, columns, 2 * LANES)

    pairs = jnp.where(far_mask == 1, tile_map, middle).reshape(-1)
    lines = lines // 2
    shape = (boxes * 2 * illum, unknowns)
    neighbours = [[first * near + d for d in range(near)] for first in range(2)]
    steps = 4

    def translate(v):
        return pl.pallas_call(
            functools.partial(translate_kernel, wide, slab, sub, rows, columns),
            grid_spec=pltpu.PrefetchScalarGridSpec(
                num_scalar_prefetch=1,
                grid=(half // steps,),
                in_specs=[
                    pl.BlockSpec(block, lambda k, pairs: (0, 0, 0, 0, 0)),
                    pl.BlockSpec(
                        (1, 2, steps, count, columns, 2 * LANES), lambda k, pairs: (v, 0, k, 0, 0, 0)
                    ),
                ],
                out_specs=pl.BlockSpec((near,) + block[1:], lambda k, pairs: (0, 0, 0, 0, 0)),
            ),
            out_shape=jax.ShapeDtypeStruct((near,) + block[1:], jnp.bfloat16),
            compiler_params=params,
            name="translate",
        )(pairs, received, expanded)

    def exchange(values):
        return lax.all_to_all(
            values, OWNERS, split_axis=0, concat_axis=0, tiled=True, axis_index_groups=neighbours
        )

    def field(values, kind):
        return pl.pallas_call(
            functools.partial(field_kernel, boxes, illum),
            out_shape=jax.ShapeDtypeStruct(shape, kind),
            scratch_shapes=[
                pltpu.VMEM((near * half * PITCH, LANES), jnp.float32),
                pltpu.VMEM((boxes * PITCH, unknowns), jnp.float32),
            ],
            compiler_params=params,
            name="field",
        )(values.reshape(lines, LANES), pattern)

    far_half = exchange(translate(0))
    near_half = exchange(translate(1))
    across = lax.ppermute(
        field(far_half, jnp.bfloat16), "wide", [(w, (w + wide // 2) % wide) for w in range(wide)]
    )
    total = field(near_half, jnp.float32) + across.astype(jnp.float32)
    return total.astype(jnp.bfloat16).reshape(source.shape)


def aggregate(values, pattern_real, pattern_imag):

    def product(left_side, right_side):
        return jnp.einsum(
            "axrp,kp->krax", left_side, right_side, preferred_element_type=jnp.float32
        )

    values_real = values[:, :, 0]
    values_imag = values[:, :, 1]
    out_real = product(values_real, pattern_real) - product(values_imag, pattern_imag)
    out_imag = product(values_real, pattern_imag) + product(values_imag, pattern_real)
    return jnp.stack([out_real, out_imag], axis=1).astype(jnp.bfloat16)


def general_local(source, aggregation, translators, tile_map, far_mask, box_offsets, disaggregation):
    own_rows = source.shape[0]
    tile_count = translators.shape[2]
    offset_count = translators.shape[3]
    box_count = box_offsets.shape[0]
    target_block = 2
    block_count = own_rows // target_block
    outgoing = lax.all_to_all(
        aggregate(source, aggregation[0], aggregation[1]),
        "wide",
        split_axis=0,
        concat_axis=4,
        tiled=True,
    )
    directions_here = outgoing.shape[0]
    illum_here = outgoing.shape[2]
    row_table = jnp.concatenate(
        [translators, jnp.zeros((2, directions_here, 1, offset_count), jnp.bfloat16)], axis=2
    )
    offset_ids = lax.broadcasted_iota(jnp.int32, (offset_count, box_count, box_count), 0)
    selector = (offset_ids == box_offsets[None, :, :]).astype(jnp.bfloat16)
    selector = selector.reshape(offset_count, box_count * box_count)

    def translate(target_first, source_first, source_block):
        source_count = source_block.shape[3]
        pair_map = lax.dynamic_slice(
            tile_map, (target_first, source_first), (target_block, source_count)
        )
        pair_far = lax.dynamic_slice(
            far_mask, (target_first, source_first), (target_block, source_count)
        )
        pair_index = jnp.where(pair_far == 1, pair_map, tile_count)
        pair_rows = jnp.take(row_table, pair_index.reshape(-1), axis=2)
        expanded = jnp.dot(
            pair_rows.reshape(-1, offset_count), selector, preferred_element_type=jnp.float32
        )
        coupling = expanded.astype(jnp.bfloat16).reshape(
            2, directions_here, target_block, source_count, box_count, box_count
        )
        values = source_block.reshape(directions_here, 2 * illum_here, source_count, box_count)
        combos = jnp.einsum(
            "klcy,qkacxy->klqax", values, coupling, preferred_element_type=jnp.float32
        )
        combos = combos.reshape(directions_here, 2, illum_here, 2, target_block * box_count)
        incoming_real = combos[:, 0, :, 0] - combos[:, 1, :, 1]
        incoming_imag = combos[:, 1, :, 0] + combos[:, 0, :, 1]
        return jnp.stack([incoming_real, incoming_imag], axis=1)

    slab_first = lax.axis_index("slab") * own_rows

    def block_rows(block_index):
        return translate(block_index * target_block, slab_first, outgoing)

    summed = lax.psum_scatter(
        lax.map(block_rows, jnp.arange(block_count * lax.axis_size("slab"), dtype=jnp.int32)),
        "slab",
        scatter_dimension=0,
        tiled=True,
    )
    incoming = summed.astype(jnp.bfloat16)
    incoming = incoming.reshape(incoming.shape[:4] + (target_block, box_count))
    item_rows = lax.all_to_all(incoming, "wide", split_axis=5, concat_axis=1, tiled=True)

    def product(left_side, right_side):
        return jnp.einsum(
            "bkrax,pk->baxrp", left_side, right_side, preferred_element_type=jnp.float32
        )

    items_real = item_rows[:, :, 0]
    items_imag = item_rows[:, :, 1]
    field_real = product(items_real, disaggregation[0]) - product(items_imag, disaggregation[1])
    field_imag = product(items_real, disaggregation[1]) + product(items_imag, disaggregation[0])
    stacked = jnp.stack([field_real, field_imag], axis=3).astype(jnp.bfloat16)
    return stacked.reshape((stacked.shape[0] * stacked.shape[1],) + stacked.shape[2:])


def local(wide, slab, sub, *args):
    source, aggregation, translators, _, _, box_offsets, _ = args
    rows, columns, _, illum, unknowns = source.shape
    share = aggregation.shape[1] // (wide * slab * sub)
    tiles = (
        2 * rows * columns == LANES
        and 2 * box_offsets.shape[0] == LANES
        and columns * wide == box_offsets.shape[0]
        and slab == 2
        and wide == 4
        and columns == 16
        and illum == 16
        and share % 32 == 0
        and unknowns == LANES
        and LANES < translators.shape[3] <= 2 * LANES
        and translators.shape[2] <= 32
    )
    if tiles:
        return tiled_local(wide, slab, sub, *args)
    return general_local(*args)


def solution(mesh):
    placed = (
        P(("groups", "slab"), "wide", None, "sub", None),
        P(None, "groups", None),
        P(None, ("groups", "wide"), None, None),
        P(),
        P(),
        P(),
        P(None, None, "groups"),
    )
    return jax.shard_map(
        functools.partial(local, mesh.shape["wide"], mesh.shape["slab"], mesh.shape["sub"]),
        mesh=mesh,
        in_specs=placed,
        out_specs=P(("groups", "slab"), "wide", None, "sub", None),
        check_vma=False,
    )
```

profile of v0, /device:TPU:0, one launch (start us, length us, event | category | flops | bytes accessed | tf_op | source)
XLA Modules:
  0.0 124.9 jit_solution(10704467582255405616)
XLA Ops:
  0.0 5.1 %outgoing.1 = bf16[8192,128]{1,0:T(8,128)(2,1)} custom-call(bf16[2048,128]{1,0:T(8,128)(2,1)} %bitcast.20, bf16[2,512,128]{2,1,0:T(8,128)(2,1)} %agg_ref.1), custom_call_target="tpu_custom_call" | custom-call | tf_op jit(solution)/shard_map/outgoing/pallas_call | solution.py:212
  5.1 7.4 %all-to-all-start = ((bf16[16,16,2,16,128]{4,3,2,1,0:T(8,128)(2,1)}), bf16[16,16,2,16,128]{4,3,2,1,0:T(8,128)(2,1)S(1)}, u32[]{:S(2)}, u32[]{:S(2)}) async-start(bf16[16,16,2,16,128]{4,3,2,1,0:T(8,128)(2,1)} %bitcast.17), calls=%async_computation | async-start | bytes 4194304 | tf_op jit(solution)/shard_map/all_to_all | solution.py:223
  12.5 1.7 %pattern.1.pattern_ref = bf16[256,512]{1,0:T(8,128)(2,1)} custom-call(s32[1]{0:T(128)} %bitcast.6.place_ref, bf16[2,128,512]{2,1,0:T(8,128)(2,1)} %dis_ref.1), custom_call_target="tpu_custom_call" | custom-call | tf_op jit(solution)/shard_map/pattern/pallas_call | solution.py:233
  14.2 0.0 copy-done.3
  14.2 0.7 pad_add_fusion.index_ref
  14.9 8.0 %copy.10.table_ref = bf16[2,128,31,255]{3,2,1,0:T(8,128)(2,1)} copy(bf16[2,128,31,255]{1,0,3,2:T(2,128)(2,1)} %param.9) | data formatting | bytes 8094720 | tf_op args[2]
  22.9 0.0 copy-done.4
  22.9 0.6 reshape.35.pair_ref
  23.5 11.5 %expand.1 = bf16[2,32,31,16,256]{4,3,2,1,0:T(8,128)(2,1)} custom-call(s32[1]{0:T(128)} %bitcast.2.base_ref, s32[32,128]{1,0:T(8,128)} %pad_add_fusion.index_ref, bf16[2,128,31,255]{3,2,1,0:T(8,128)(2,1)} %copy.10.table_ref), custom_call_target="tpu_custom_call" | custom-call | tf_op jit(solution)/shard_map/expand/pallas_call | solution.py:247
  35.0 18.6 %all-to-all-done.src_ref = bf16[16,16,2,16,128]{4,3,2,1,0:T(8,128)(2,1)S(1)} async-done(((bf16[16,16,2,16,128]{4,3,2,1,0:T(8,128)(2,1)}), bf16[16,16,2,16,128]{4,3,2,1,0:T(8,128)(2,1)S(1)}, u32[]{:S(2)}, u32[]{:S(2)}) %all-to-all-start) | async-done | bytes 2097184 | tf_op jit(solution)/shard_map/all_to_all | solution.py:223
  53.6 1.3 %copy-done = bf16[16,16,2,16,128]{4,3,2,1,0:T(8,128)(2,1)} copy-done((bf16[16,16,2,16,128]{4,3,2,1,0:T(8,128)(2,1)}, bf16[16,16,2,16,128]{4,3,2,1,0:T(8,128)(2,1)S(1)}, u32[]{:S(2)}) %copy-start) | copy-done | bytes 2097176
  54.9 9.9 %translate.3 = bf16[8,16,2,16,128]{4,3,2,1,0:T(8,128)(2,1)} custom-call(s32[64]{0:T(128)} %reshape.35.pair_ref, bf16[16,16,2,16,128]{4,3,2,1,0:T(8,128)(2,1)} %copy-done, bf16[2,2,16,31,16,256]{5,4,3,2,1,0:T(8,128)(2,1)} %bitcast.15), custom_call_target="tpu_custom_call" | custom-call | tf_op jit(solution)/shard_map/translate/pallas_call | solution.py:280
  64.8 10.3 %all-to-all-start.2 = ((bf16[8,16,2,16,128]{4,3,2,1,0:T(8,128)(2,1)}), bf16[8,16,2,16,128]{4,3,2,1,0:T(8,128)(2,1)S(1)}, u32[]{:S(2)}, u32[]{:S(2)}) async-start(bf16[8,16,2,16,128]{4,3,2,1,0:T(8,128)(2,1)} %translate.3), calls=%async_computation.2 | async-start | bytes 2097152 | tf_op jit(solution)/shard_map/all_to_all | solution.py:299
  75.1 9.9 %translate.2 = bf16[8,16,2,16,128]{4,3,2,1,0:T(8,128)(2,1)} custom-call(s32[64]{0:T(128)} %reshape.35.pair_ref, bf16[16,16,2,16,128]{4,3,2,1,0:T(8,128)(2,1)} %copy-done, bf16[2,2,16,31,16,256]{5,4,3,2,1,0:T(8,128)(2,1)} %bitcast.16), custom_call_target="tpu_custom_call" | custom-call | tf_op jit(solution)/shard_map/translate/pallas_call | solution.py:280
  85.0 4.6 %all-to-all-done.2 = bf16[8,16,2,16,128]{4,3,2,1,0:T(8,128)(2,1)S(1)} async-done(((bf16[8,16,2,16,128]{4,3,2,1,0:T(8,128)(2,1)}), bf16[8,16,2,16,128]{4,3,2,1,0:T(8,128)(2,1)S(1)}, u32[]{:S(2)}, u32[]{:S(2)}) %all-to-all-start.2) | async-done | bytes 1048608 | tf_op jit(solution)/shard_map/all_to_all | solution.py:299
  89.5 3.6 %all-to-all-start.1 = ((bf16[8,16,2,16,128]{4,3,2,1,0:T(8,128)(2,1)}), bf16[8,16,2,16,128]{4,3,2,1,0:T(8,128)(2,1)S(1)}, u32[]{:S(2)}, u32[]{:S(2)}) async-start(bf16[8,16,2,16,128]{4,3,2,1,0:T(8,128)(2,1)} %translate.2), calls=%async_computation.1 | async-start | bytes 2097152 | tf_op jit(solution)/shard_map/all_to_all | solution.py:299
  93.1 0.0 copy-done.1
  93.1 3.0 %field.3 = bf16[2048,128]{1,0:T(8,128)(2,1)} custom-call(bf16[4096,128]{1,0:T(8,128)(2,1)} %bitcast.18, bf16[256,512]{1,0:T(8,128)(2,1)} %pattern.1.pattern_ref), custom_call_target="tpu_custom_call" | custom-call | tf_op jit(solution)/shard_map/field/pallas_call | solution.py:304
  96.1 2.6 %collective-permute-start = (bf16[2048,128]{1,0:T(8,128)(2,1)}, bf16[2048,128]{1,0:T(8,128)(2,1)S(1)}, u32[]{:S(2)}, u32[]{:S(2)}) collective-permute-start(bf16[2048,128]{1,0:T(8,128)(2,1)} %field.3), channel_id=1, source_target_pairs={{0,8},{4,12},{8,0},{12,4},{1,9},{5,13},{9,1},{13,5},{2,10},{6,14},... | collective-permute-start | bytes 1572872 | tf_op jit(solution)/shard_map/ppermute | solution.py:317
  98.7 18.1 %all-to-all-done.1 = bf16[8,16,2,16,128]{4,3,2,1,0:T(8,128)(2,1)S(1)} async-done(((bf16[8,16,2,16,128]{4,3,2,1,0:T(8,128)(2,1)}), bf16[8,16,2,16,128]{4,3,2,1,0:T(8,128)(2,1)S(1)}, u32[]{:S(2)}, u32[]{:S(2)}) %all-to-all-start.1) | async-done | bytes 1048608 | tf_op jit(solution)/shard_map/all_to_all | solution.py:299
  116.8 1.0 copy-done.2
  117.8 3.3 %field.2 = f32[2048,128]{1,0:T(8,128)} custom-call(bf16[4096,128]{1,0:T(8,128)(2,1)} %bitcast.19, bf16[256,512]{1,0:T(8,128)(2,1)} %pattern.1.pattern_ref), custom_call_target="tpu_custom_call" | custom-call | tf_op jit(solution)/shard_map/field/pallas_call | solution.py:304
  121.1 1.7 %collective-permute-done = bf16[2048,128]{1,0:T(8,128)(2,1)S(1)} collective-permute-done((bf16[2048,128]{1,0:T(8,128)(2,1)}, bf16[2048,128]{1,0:T(8,128)(2,1)S(1)}, u32[]{:S(2)}, u32[]{:S(2)}) %collective-permute-start) | collective-permute-done | bytes 524320 | tf_op jit(solution)/shard_map/ppermute | solution.py:317
  122.8 2.1 %add_convert_fusion = bf16[2048,128]{1,0:T(8,128)(2,1)} fusion(f32[2048,128]{1,0:T(8,128)} %field.2, bf16[2048,128]{1,0:T(8,128)(2,1)S(1)} %collective-permute-done), kind=kLoop, calls=%fused_computation | loop fusion | flops 786432 | bytes 2097152 | tf_op jit(solution)/shard_map/convert_element_type | solution.py:321
  (11 shorter events, 0.0 us)
Async XLA Ops:
  0.0 14.2 %copy-start.3 = (s32[64,64]{1,0:T(8,128)S(1)}, s32[64,64]{1,0:T(8,128)}, u32[]{:S(2)}) copy-start(s32[64,64]{1,0:T(8,128)} %param.12) | copy-start | bytes 49156
  5.1 48.5 %all-to-all-start = ((bf16[16,16,2,16,128]{4,3,2,1,0:T(8,128)(2,1)}), bf16[16,16,2,16,128]{4,3,2,1,0:T(8,128)(2,1)S(1)}, u32[]{:S(2)}, u32[]{:S(2)}) async-start(bf16[16,16,2,16,128]{4,3,2,1,0:T(8,128)(2,1)} %bitcast.17), calls=%async_computation | async-start | bytes 4194304 | tf_op jit(solution)/shard_map/all_to_all | solution.py:223
  14.9 8.0 %copy-start.4 = (s32[8,8]{1,0:T(8,128)S(1)}, s32[8,8]{1,0:T(8,128)}, u32[]{:S(2)}) copy-start(s32[8,8]{1,0:T(8,128)} %param.10) | copy-start | bytes 772
  14.9 8.0 %copy-start.5 = (s32[8,8]{1,0:T(8,128)S(1)}, s32[8,8]{1,0:T(8,128)}, u32[]{:S(2)}) copy-start(s32[8,8]{1,0:T(8,128)} %param.11) | copy-start | bytes 772
  53.6 1.3 %copy-start = (bf16[16,16,2,16,128]{4,3,2,1,0:T(8,128)(2,1)}, bf16[16,16,2,16,128]{4,3,2,1,0:T(8,128)(2,1)S(1)}, u32[]{:S(2)}) copy-start(bf16[16,16,2,16,128]{4,3,2,1,0:T(8,128)(2,1)S(1)} %all-to-all-done.src_ref) | copy-start | bytes 6291460
  64.8 24.7 %all-to-all-start.2 = ((bf16[8,16,2,16,128]{4,3,2,1,0:T(8,128)(2,1)}), bf16[8,16,2,16,128]{4,3,2,1,0:T(8,128)(2,1)S(1)}, u32[]{:S(2)}, u32[]{:S(2)}) async-start(bf16[8,16,2,16,128]{4,3,2,1,0:T(8,128)(2,1)} %translate.3), calls=%async_computation.2 | async-start | bytes 2097152 | tf_op jit(solution)/shard_map/all_to_all | solution.py:299
  89.5 3.6 %copy-start.1 = (bf16[8,16,2,16,128]{4,3,2,1,0:T(8,128)(2,1)}, bf16[8,16,2,16,128]{4,3,2,1,0:T(8,128)(2,1)S(1)}, u32[]{:S(2)}) copy-start(bf16[8,16,2,16,128]{4,3,2,1,0:T(8,128)(2,1)S(1)} %all-to-all-done.2) | copy-start | bytes 3145732
  89.5 27.3 %all-to-all-start.1 = ((bf16[8,16,2,16,128]{4,3,2,1,0:T(8,128)(2,1)}), bf16[8,16,2,16,128]{4,3,2,1,0:T(8,128)(2,1)S(1)}, u32[]{:S(2)}, u32[]{:S(2)}) async-start(bf16[8,16,2,16,128]{4,3,2,1,0:T(8,128)(2,1)} %translate.2), calls=%async_computation.1 | async-start | bytes 2097152 | tf_op jit(solution)/shard_map/all_to_all | solution.py:299
  96.1 26.6 %collective-permute-start = (bf16[2048,128]{1,0:T(8,128)(2,1)}, bf16[2048,128]{1,0:T(8,128)(2,1)S(1)}, u32[]{:S(2)}, u32[]{:S(2)}) collective-permute-start(bf16[2048,128]{1,0:T(8,128)(2,1)} %field.3), channel_id=1, source_target_pairs={{0,8},{4,12},{8,0},{12,4},{1,9},{5,13},{9,1},{13,5},{2,10},{6,14},... | collective-permute-start | bytes 1572872 | tf_op jit(solution)/shard_map/ppermute | solution.py:317
  116.8 1.0 copy-start.2
where the time goes:
time: 126 us; the launch traced here: 125 us
  Pallas kernels  44.4 us (35%)
  waiting for transfers between devices  42.9 us (34%)
  starting transfers between devices  23.8 us (19%)
  local copies, waits for them, and re-layouts  10.9 us (9%)
  other arithmetic  2.81 us (2%)
    all_to_all x2, waiting for transfers between devices, exchange(): lax.all_to_all(values, OWNERS, split_axis=0, concat_axis=0, tiled=True, a...  22.6 us
    pallas_call x2, Pallas kernels, translate(): pl.pallas_call(functools.partial(translate_kernel, wide, slab, sub, rows,...  19.8 us
    all_to_all x1, waiting for transfers between devices, tiled_local(): lax.all_to_all(outgoing.reshape(block), OWNERS, split_axis=0, concat_axis...  18.6 us
    all_to_all x2, starting transfers between devices, exchange(): lax.all_to_all(values, OWNERS, split_axis=0, concat_axis=0, tiled=True, a...  13.8 us
    pallas_call x1, Pallas kernels, tiled_local(): pl.pallas_call(functools.partial(expand_kernel, middle), grid_spec=pltpu....  11.5 us
    unnamed x13, local copies, waits for them, and re-layouts  10.3 us
    all_to_all x1, starting transfers between devices, tiled_local(): lax.all_to_all(outgoing.reshape(block), OWNERS, split_axis=0, concat_axis...  7.37 us
    pallas_call x2, Pallas kernels, field(): pl.pallas_call(functools.partial(field_kernel, boxes, illum), out_shape=j...  6.35 us
  transfers between devices with their start and end apart: 4, of which 4 were waited for; matrix products, arithmetic and copies ran while one was open for 7% of the time, Pallas kernels for 24%

commit v1 on v0

--- a/solution.py
+++ b/solution.py
@@ -9,7 +9,7 @@
 
 OWNERS = ("wide", "slab", "sub")
 LANES = 128
-VMEM = 56 * 1024 * 1024
+MIB = 1024 * 1024
 PITCH = 36
 NT = (((1,), (1,)), ((), ()))
 TN = (((0,), (0,)), ((), ()))
@@ -206,7 +206,6 @@
     count = translators.shape[2]
     offsets = translators.shape[3]
     middle = count // 2
-    params = pltpu.CompilerParams(vmem_limit_bytes=VMEM)
 
     lines = devices * half * 2 * illum
     outgoing = pl.pallas_call(
@@ -216,7 +215,7 @@
             pltpu.VMEM((boxes * 2 * illum, unknowns), jnp.float32),
             pltpu.VMEM((devices * half * PITCH, LANES), jnp.float32),
         ],
-        compiler_params=params,
+        compiler_params=pltpu.CompilerParams(vmem_limit_bytes=56 * MIB),
         name="outgoing",
     )(source.reshape(boxes * 2 * illum, unknowns), aggregation)
     block = (devices, half, 2, illum, LANES)
@@ -239,7 +238,7 @@
             out_specs=pl.BlockSpec((2 * near * half, 4 * unknowns), lambda i, place: (0, 0)),
         ),
         out_shape=jax.ShapeDtypeStruct((2 * near * half, 4 * unknowns), jnp.bfloat16),
-        compiler_params=params,
+        compiler_params=pltpu.CompilerParams(vmem_limit_bytes=8 * MIB),
         name="pattern",
     )(place.reshape(1), disaggregation)
     index, pattern = lax.optimization_barrier((index, pattern))
@@ -265,7 +264,7 @@
             ],
         ),
         out_shape=jax.ShapeDtypeStruct((2, 2 * half, count, columns, 2 * LANES), jnp.bfloat16),
-        compiler_params=params,
+        compiler_params=pltpu.CompilerParams(vmem_limit_bytes=56 * MIB),
         name="expand",
     )(base.reshape(1), index, translators)
     expanded = expanded.reshape(2, 2, half, count, columns, 2 * LANES)
@@ -291,7 +290,7 @@
                 out_specs=pl.BlockSpec((near,) + block[1:], lambda k, pairs: (0, 0, 0, 0, 0)),
             ),
             out_shape=jax.ShapeDtypeStruct((near,) + block[1:], jnp.bfloat16),
-            compiler_params=params,
+            compiler_params=pltpu.CompilerParams(vmem_limit_bytes=50 * MIB),
             name="translate",
         )(pairs, received, expanded)
 
@@ -308,7 +307,7 @@
                 pltpu.VMEM((near * half * PITCH, LANES), jnp.float32),
                 pltpu.VMEM((boxes * PITCH, unknowns), jnp.float32),
             ],
-            compiler_params=params,
+            compiler_params=pltpu.CompilerParams(vmem_limit_bytes=12 * MIB),
             name="field",
         )(values.reshape(lines, LANES), pattern)
 

time: 126 us -> 119 us (0.944)
  Pallas kernels: 44.4 us -> 37 us
  waiting for transfers between devices: 42.9 us -> 47.9 us
  local copies, waits for them, and re-layouts: 10.9 us -> 8.08 us
    all_to_all x2, waiting for transfers between devices: 22.6 us -> 27.3 us  [exchange(): lax.all_to_all(values, OWNERS, split_axis=0, concat_axis=0, tiled=True, a...]
    pallas_call x2, Pallas kernels: 6.35 us -> 2.03 us  [field(): pl.pallas_call(functools.partial(field_kernel, boxes, illum), out_shape=j...]
    unnamed x13 -> x9, local copies, waits for them, and re-layouts: 10.3 us -> 7.99 us
    all_to_all x1, waiting for transfers between devices: 18.6 us -> 20.6 us  [tiled_local(): lax.all_to_all(outgoing.reshape(block), OWNERS, split_axis=0, concat_axis...]
    ppermute x1, waiting for transfers between devices: 1.65 us -> 0.01 us  [tiled_local(): lax.ppermute(field(far_half, jnp.bfloat16), 'wide', [(w, (w + wide // 2)...]
    pallas_call x1, Pallas kernels: 1.71 us -> 0.1 us  [tiled_local(): pl.pallas_call(functools.partial(pattern_kernel, near, half), grid_spec=p...]
    pallas_call x2, Pallas kernels: 19.8 us -> 18.3 us  [translate(): pl.pallas_call(functools.partial(translate_kernel, wide, slab, sub, rows,...]
  transfers between devices with their start and end apart: 4 -> 4, of which waited for: 4 -> 3; matrix products, arithmetic and copies ran while one was open for 7% -> 7% of each run, Pallas kernels for 24% -> 19%
where the time goes in v1:
time: 119 us
  waiting for transfers between devices  47.9 us (40%)
  Pallas kernels  37 us (31%)
  starting transfers between devices  23.8 us (20%)
  local copies, waits for them, and re-layouts  8.08 us (7%)
  other arithmetic  1.59 us (1%)
    all_to_all x2, waiting for transfers between devices, exchange(): lax.all_to_all(values, OWNERS, split_axis=0, concat_axis=0, tiled=True, a...  27.3 us
    all_to_all x1, waiting for transfers between devices, tiled_local(): lax.all_to_all(outgoing.reshape(block), OWNERS, split_axis=0, concat_axis...  20.6 us
    pallas_call x2, Pallas kernels, translate(): pl.pallas_call(functools.partial(translate_kernel, wide, slab, sub, rows,...  18.3 us
    all_to_all x2, starting transfers between devices, exchange(): lax.all_to_all(values, OWNERS, split_axis=0, concat_axis=0, tiled=True, a...  13.8 us
    pallas_call x1, Pallas kernels, tiled_local(): pl.pallas_call(functools.partial(expand_kernel, middle), grid_spec=pltpu....  11.5 us
    unnamed x9, local copies, waits for them, and re-layouts  7.99 us
    all_to_all x1, starting transfers between devices, tiled_local(): lax.all_to_all(outgoing.reshape(block), OWNERS, split_axis=0, concat_axis...  7.36 us
    pallas_call x1, Pallas kernels, tiled_local(): pl.pallas_call(functools.partial(outgoing_kernel, boxes, illum, devices,...  5.1 us
  transfers between devices with their start and end apart: 4, of which 3 were waited for; matrix products, arithmetic and copies ran while one was open for 7% of the time, Pallas kernels for 19%

profile of v1, /device:TPU:0, one launch (start us, length us, event | category | flops | bytes accessed | tf_op | source)
XLA Modules:
  0.0 118.6 jit_solution(4317337216052729099)
XLA Ops:
  0.0 0.0 copy-start
  0.0 5.1 %outgoing.1 = bf16[8192,128]{1,0:T(8,128)(2,1)} custom-call(bf16[2048,128]{1,0:T(8,128)(2,1)} %bitcast.20, bf16[2,512,128]{2,1,0:T(8,128)(2,1)} %agg_ref.1), custom_call_target="tpu_custom_call" | custom-call | tf_op jit(solution)/shard_map/outgoing/pallas_call | solution.py:211
  5.1 7.4 %all-to-all-start = ((bf16[16,16,2,16,128]{4,3,2,1,0:T(8,128)(2,1)}), bf16[16,16,2,16,128]{4,3,2,1,0:T(8,128)(2,1)S(1)}, u32[]{:S(2)}, u32[]{:S(2)}) async-start(bf16[16,16,2,16,128]{4,3,2,1,0:T(8,128)(2,1)} %bitcast.19), calls=%async_computation | async-start | bytes 4194304 | tf_op jit(solution)/shard_map/all_to_all | solution.py:222
  12.5 0.0 copy-done
  12.5 0.1 pattern.1.pattern_ref
  12.6 0.0 copy-done.1
  12.7 0.7 pad_add_fusion.index_ref
  13.3 8.0 %copy.10.table_ref = bf16[2,128,31,255]{3,2,1,0:T(8,128)(2,1)} copy(bf16[2,128,31,255]{1,0,3,2:T(2,128)(2,1)} %param.9) | data formatting | bytes 8094720 | tf_op args[2]
  21.3 0.0 copy-done.2
  21.3 0.0 copy-done.3
  21.3 0.1 reshape.35.pair_ref
  21.4 11.5 %expand.1 = bf16[2,32,31,16,256]{4,3,2,1,0:T(8,128)(2,1)} custom-call(s32[1]{0:T(128)} %bitcast.2.base_ref, s32[32,128]{1,0:T(8,128)} %pad_add_fusion.index_ref, bf16[2,128,31,255]{3,2,1,0:T(8,128)(2,1)} %copy.10.table_ref), custom_call_target="tpu_custom_call" | custom-call | tf_op jit(solution)/shard_map/expand/pallas_call | solution.py:246
  32.9 20.6 %all-to-all-done.src_ref = bf16[16,16,2,16,128]{4,3,2,1,0:T(8,128)(2,1)S(1)} async-done(((bf16[16,16,2,16,128]{4,3,2,1,0:T(8,128)(2,1)}), bf16[16,16,2,16,128]{4,3,2,1,0:T(8,128)(2,1)S(1)}, u32[]{:S(2)}, u32[]{:S(2)}) %all-to-all-start) | async-done | bytes 2097184 | tf_op jit(solution)/shard_map/all_to_all | solution.py:222
  53.6 9.1 %translate.3 = bf16[8,16,2,16,128]{4,3,2,1,0:T(8,128)(2,1)} custom-call(s32[64]{0:T(128)S(1)} %reshape.35.pair_ref, bf16[16,16,2,16,128]{4,3,2,1,0:T(8,128)(2,1)S(1)} %all-to-all-done.src_ref, bf16[2,2,16,31,16,256]{5,4,3,2,1,0:T(8,128)(2,1)} %bitcast.17), custom_call_target="tpu_custom_call" | custom-call | tf_op jit(solution)/shard_map/translate/pallas_call | solution.py:279
  62.7 10.3 %all-to-all-start.2 = ((bf16[8,16,2,16,128]{4,3,2,1,0:T(8,128)(2,1)}), bf16[8,16,2,16,128]{4,3,2,1,0:T(8,128)(2,1)S(1)}, u32[]{:S(2)}, u32[]{:S(2)}) async-start(bf16[8,16,2,16,128]{4,3,2,1,0:T(8,128)(2,1)} %translate.3), calls=%async_computation.2 | async-start | bytes 2097152 | tf_op jit(solution)/shard_map/all_to_all | solution.py:298
  73.0 9.1 %translate.2 = bf16[8,16,2,16,128]{4,3,2,1,0:T(8,128)(2,1)} custom-call(s32[64]{0:T(128)S(1)} %reshape.35.pair_ref, bf16[16,16,2,16,128]{4,3,2,1,0:T(8,128)(2,1)S(1)} %all-to-all-done.src_ref, bf16[2,2,16,31,16,256]{5,4,3,2,1,0:T(8,128)(2,1)} %bitcast.18), custom_call_target="tpu_custom_call" | custom-call | tf_op jit(solution)/shard_map/translate/pallas_call | solution.py:279
  82.1 5.3 %all-to-all-done.2 = bf16[8,16,2,16,128]{4,3,2,1,0:T(8,128)(2,1)S(1)} async-done(((bf16[8,16,2,16,128]{4,3,2,1,0:T(8,128)(2,1)}), bf16[8,16,2,16,128]{4,3,2,1,0:T(8,128)(2,1)S(1)}, u32[]{:S(2)}, u32[]{:S(2)}) %all-to-all-start.2) | async-done | bytes 1048608 | tf_op jit(solution)/shard_map/all_to_all | solution.py:298
  87.4 3.6 %all-to-all-start.1 = ((bf16[8,16,2,16,128]{4,3,2,1,0:T(8,128)(2,1)}), bf16[8,16,2,16,128]{4,3,2,1,0:T(8,128)(2,1)S(1)}, u32[]{:S(2)}, u32[]{:S(2)}) async-start(bf16[8,16,2,16,128]{4,3,2,1,0:T(8,128)(2,1)} %translate.2), calls=%async_computation.1 | async-start | bytes 2097152 | tf_op jit(solution)/shard_map/all_to_all | solution.py:298
  91.0 1.0 field.3
  92.0 2.6 %collective-permute-start = (bf16[2048,128]{1,0:T(8,128)(2,1)S(1)}, bf16[2048,128]{1,0:T(8,128)(2,1)S(1)}, u32[]{:S(2)}, u32[]{:S(2)}) collective-permute-start(bf16[2048,128]{1,0:T(8,128)(2,1)S(1)} %field.3), channel_id=1, source_target_pairs={{0,8},{4,12},{8,0},{12,4},{1,9},{5,13},{9,1},{13,5},{2,10},{6,14},... | collective-permute-start | bytes 1572872 | tf_op jit(solution)/shard_map/ppermute | solution.py:316
  94.6 22.0 %all-to-all-done.1 = bf16[8,16,2,16,128]{4,3,2,1,0:T(8,128)(2,1)S(1)} async-done(((bf16[8,16,2,16,128]{4,3,2,1,0:T(8,128)(2,1)}), bf16[8,16,2,16,128]{4,3,2,1,0:T(8,128)(2,1)S(1)}, u32[]{:S(2)}, u32[]{:S(2)}) %all-to-all-start.1) | async-done | bytes 1048608 | tf_op jit(solution)/shard_map/all_to_all | solution.py:298
  116.6 1.1 field.2
  117.7 0.0 collective-permute-done
  117.7 0.9 add_convert_fusion
  (7 shorter events, 0.0 us)
Async XLA Ops:
  0.0 12.5 %copy-start = (bf16[2,128,512]{2,1,0:T(8,128)(2,1)S(1)}, bf16[2,128,512]{2,1,0:T(8,128)(2,1)}, u32[]{:S(2)}) copy-start(bf16[2,128,512]{2,1,0:T(8,128)(2,1)} %dis_ref.1) | copy-start | bytes 786436
  0.0 12.6 %copy-start.1 = (s32[64,64]{1,0:T(8,128)S(1)}, s32[64,64]{1,0:T(8,128)}, u32[]{:S(2)}) copy-start(s32[64,64]{1,0:T(8,128)} %param.12) | copy-start | bytes 49156
  5.1 48.5 %all-to-all-start = ((bf16[16,16,2,16,128]{4,3,2,1,0:T(8,128)(2,1)}), bf16[16,16,2,16,128]{4,3,2,1,0:T(8,128)(2,1)S(1)}, u32[]{:S(2)}, u32[]{:S(2)}) async-start(bf16[16,16,2,16,128]{4,3,2,1,0:T(8,128)(2,1)} %bitcast.19), calls=%async_computation | async-start | bytes 4194304 | tf_op jit(solution)/shard_map/all_to_all | solution.py:222
  13.3 8.0 %copy-start.2 = (s32[8,8]{1,0:T(8,128)S(1)}, s32[8,8]{1,0:T(8,128)}, u32[]{:S(2)}) copy-start(s32[8,8]{1,0:T(8,128)} %param.10) | copy-start | bytes 772
  13.3 8.0 %copy-start.3 = (s32[8,8]{1,0:T(8,128)S(1)}, s32[8,8]{1,0:T(8,128)}, u32[]{:S(2)}) copy-start(s32[8,8]{1,0:T(8,128)} %param.11) | copy-start | bytes 772
  62.7 24.7 %all-to-all-start.2 = ((bf16[8,16,2,16,128]{4,3,2,1,0:T(8,128)(2,1)}), bf16[8,16,2,16,128]{4,3,2,1,0:T(8,128)(2,1)S(1)}, u32[]{:S(2)}, u32[]{:S(2)}) async-start(bf16[8,16,2,16,128]{4,3,2,1,0:T(8,128)(2,1)} %translate.3), calls=%async_computation.2 | async-start | bytes 2097152 | tf_op jit(solution)/shard_map/all_to_all | solution.py:298
  87.4 29.2 %all-to-all-start.1 = ((bf16[8,16,2,16,128]{4,3,2,1,0:T(8,128)(2,1)}), bf16[8,16,2,16,128]{4,3,2,1,0:T(8,128)(2,1)S(1)}, u32[]{:S(2)}, u32[]{:S(2)}) async-start(bf16[8,16,2,16,128]{4,3,2,1,0:T(8,128)(2,1)} %translate.2), calls=%async_computation.1 | async-start | bytes 2097152 | tf_op jit(solution)/shard_map/all_to_all | solution.py:298
  92.0 25.7 %collective-permute-start = (bf16[2048,128]{1,0:T(8,128)(2,1)S(1)}, bf16[2048,128]{1,0:T(8,128)(2,1)S(1)}, u32[]{:S(2)}, u32[]{:S(2)}) collective-permute-start(bf16[2048,128]{1,0:T(8,128)(2,1)S(1)} %field.3), channel_id=1, source_target_pairs={{0,8},{4,12},{8,0},{12,4},{1,9},{5,13},{9,1},{13,5},{2,10},{6,14},... | collective-permute-start | bytes 1572872 | tf_op jit(solution)/shard_map/ppermute | solution.py:316

commit v2 on v1

--- a/solution.py
+++ b/solution.py
@@ -15,7 +15,7 @@
 TN = (((0,), (0,)), ((), ()))
 
 
-def outgoing_kernel(boxes, illum, devices, half, src_ref, agg_ref, out_ref, wide_src, wide_out):
+def outgoing_kernel(boxes, illum, devices, half, place_ref, src_ref, agg_ref, out_ref, wide_src, wide_out):
     unknowns = src_ref.shape[1]
     wide_src[...] = src_ref[...].astype(jnp.float32)
     real = agg_ref[0].astype(jnp.float32)
@@ -88,9 +88,9 @@
                     ].astype(jnp.bfloat16)
 
 
-def translate_kernel(wide, slab, sub, rows, columns, pair_ref, src_ref, exp_ref, out_ref):
-    illum = src_ref.shape[3]
-    steps = exp_ref.shape[2]
+def translate_kernel(wide, slab, sub, rows, columns, pair_ref, own_ref, far_ref, low_ref, high_ref, out_ref):
+    illum = own_ref.shape[3]
+    steps = low_ref.shape[1]
     all_rows = slab * rows
     lane = lax.broadcasted_iota(jnp.int32, (illum, LANES), 1)
     group = lane // columns
@@ -105,7 +105,7 @@
         def turn(s, u, q, w, amount):
             key = (s, u, q, w, amount)
             if key not in turned:
-                tile = src_ref[(w * slab + s) * sub + u, here, q]
+                tile = (own_ref, far_ref)[w // 2][(w % 2 * slab + s) * sub + u, here, q]
                 turned[key] = pltpu.roll(tile, amount * columns, 1) if amount else tile
             return turned[key]
 
@@ -133,7 +133,11 @@
                         left.append(jnp.concatenate([parts[u, 1, h], parts[u, 0, h]], axis=1))
                 left = jnp.concatenate(left, axis=0)
                 right = jnp.concatenate(
-                    [exp_ref[0, k2, step, pair_ref[a * all_rows + c]] for a in range(all_rows)], axis=0
+                    [
+                        (low_ref, high_ref)[k2][0, step, pair_ref[a * all_rows + c]]
+                        for a in range(all_rows)
+                    ],
+                    axis=0,
                 )
                 product = lax.dot_general(left, right, NT, preferred_element_type=jnp.float32)
                 sums[k2] = product if sums[k2] is None else sums[k2] + product
@@ -207,28 +211,53 @@
     offsets = translators.shape[3]
     middle = count // 2
 
-    lines = devices * half * 2 * illum
-    outgoing = pl.pallas_call(
-        functools.partial(outgoing_kernel, boxes, illum, devices, half),
-        out_shape=jax.ShapeDtypeStruct((lines, LANES), jnp.bfloat16),
-        scratch_shapes=[
-            pltpu.VMEM((boxes * 2 * illum, unknowns), jnp.float32),
-            pltpu.VMEM((devices * half * PITCH, LANES), jnp.float32),
-        ],
-        compiler_params=pltpu.CompilerParams(vmem_limit_bytes=56 * MIB),
-        name="outgoing",
-    )(source.reshape(boxes * 2 * illum, unknowns), aggregation)
-    block = (devices, half, 2, illum, LANES)
-    received = lax.all_to_all(outgoing.reshape(block), OWNERS, split_axis=0, concat_axis=0, tiled=True)
+    near = devices // 2
+    lines = near * half * 2 * illum
+    block = (near, half, 2, illum, LANES)
+    shape = (boxes * 2 * illum, unknowns)
+    place = lax.axis_index("wide") // 2
+    neighbours = [[first * near + d for d in range(near)] for first in range(2)]
+
+    def exchange(values):
+        return lax.all_to_all(
+            values, OWNERS, split_axis=0, concat_axis=0, tiled=True, axis_index_groups=neighbours
+        )
+
+    def cross(values):
+        return lax.ppermute(values, "wide", [(w, (w + wide // 2) % wide) for w in range(wide)])
+
+    def outgoing(values):
+        return pl.pallas_call(
+            functools.partial(outgoing_kernel, boxes, illum, near, half),
+            grid_spec=pltpu.PrefetchScalarGridSpec(
+                num_scalar_prefetch=1,
+                grid=(1,),
+                in_specs=[
+                    pl.BlockSpec(shape, lambda i, place: (0, 0)),
+                    pl.BlockSpec((2, directions // 2, unknowns), lambda i, place: (0, place[0], 0)),
+                ],
+                out_specs=pl.BlockSpec((lines, LANES), lambda i, place: (0, 0)),
+                scratch_shapes=[
+                    pltpu.VMEM(shape, jnp.float32),
+                    pltpu.VMEM((near * half * PITCH, LANES), jnp.float32),
+                ],
+            ),
+            out_shape=jax.ShapeDtypeStruct((lines, LANES), jnp.bfloat16),
+            compiler_params=pltpu.CompilerParams(vmem_limit_bytes=56 * MIB),
+            name="outgoing",
+        )(place.reshape(1), values, aggregation).reshape(block)
+
+    flat = source.reshape(shape)
+    across_source = cross(flat)
+    own = exchange(outgoing(flat))
 
     side = box_offsets.shape[0]
     x_half = side // 2
-    place = lax.axis_index("wide") // 2
-    by_side = jnp.where(place == 0, jnp.roll(box_offsets, x_half, axis=0), box_offsets)
+    by_side = jnp.roll(box_offsets, x_half, axis=0)
+    by_side = jnp.where(place == 0, by_side, jnp.roll(box_offsets, x_half, axis=1))
     by_side = by_side.reshape(2, 2, columns, side)
     index = jnp.concatenate([by_side[:, 0], by_side[:, 1]], axis=-1).reshape(x_half, 2 * side)
     base = lax.axis_index("slab") * sub + lax.axis_index("sub")
-    near = devices // 2
     pattern = pl.pallas_call(
         functools.partial(pattern_kernel, near, half),
         grid_spec=pltpu.PrefetchScalarGridSpec(
@@ -241,38 +270,42 @@
         compiler_params=pltpu.CompilerParams(vmem_limit_bytes=8 * MIB),
         name="pattern",
     )(place.reshape(1), disaggregation)
-    index, pattern = lax.optimization_barrier((index, pattern))
+    base = lax.axis_index("slab") * sub + lax.axis_index("sub")
     batch = 4
-    expanded = pl.pallas_call(
-        functools.partial(expand_kernel, middle),
-        grid_spec=pltpu.PrefetchScalarGridSpec(
-            num_scalar_prefetch=1,
-            grid=(2 * half // batch,),
-            in_specs=[
-                pl.BlockSpec((x_half, 2 * side), lambda k, base: (0, 0)),
-                pl.BlockSpec(
-                    (2, batch, count, offsets), lambda k, base: (0, base[0] * (2 * half // batch) + k, 0, 0)
+
+    def expand(k2):
+        per_part = half // batch
+        return pl.pallas_call(
+            functools.partial(expand_kernel, middle),
+            grid_spec=pltpu.PrefetchScalarGridSpec(
+                num_scalar_prefetch=1,
+                grid=(per_part,),
+                in_specs=[
+                    pl.BlockSpec((x_half, 2 * side), lambda k, base: (0, 0)),
+                    pl.BlockSpec(
+                        (2, batch, count, offsets),
+                        lambda k, base: (0, (2 * base[0] + k2) * per_part + k, 0, 0),
+                    ),
+                ],
+                out_specs=pl.BlockSpec(
+                    (2, batch, count, columns, 2 * LANES), lambda k, base: (0, k, 0, 0, 0)
                 ),
-            ],
-            out_specs=pl.BlockSpec(
-                (2, batch, count, columns, 2 * LANES), lambda k, base: (0, k, 0, 0, 0)
+                scratch_shapes=[
+                    pltpu.VMEM((2 * LANES, x_half * LANES), jnp.bfloat16),
+                    pltpu.VMEM((2 * batch * x_half, 2 * LANES), jnp.bfloat16),
+                    pltpu.VMEM((2 * batch * x_half * PITCH, LANES), jnp.float32),
+                ],
             ),
-            scratch_shapes=[
-                pltpu.VMEM((2 * LANES, x_half * LANES), jnp.bfloat16),
-                pltpu.VMEM((2 * batch * x_half, 2 * LANES), jnp.bfloat16),
-                pltpu.VMEM((2 * batch * x_half * PITCH, LANES), jnp.float32),
-            ],
-        ),
-        out_shape=jax.ShapeDtypeStruct((2, 2 * half, count, columns, 2 * LANES), jnp.bfloat16),
-        compiler_params=pltpu.CompilerParams(vmem_limit_bytes=56 * MIB),
-        name="expand",
-    )(base.reshape(1), index, translators)
-    expanded = expanded.reshape(2, 2, half, count, columns, 2 * LANES)
-
+            out_shape=jax.ShapeDtypeStruct((2, half, count, columns, 2 * LANES), jnp.bfloat16),
+            compiler_params=pltpu.CompilerParams(vmem_limit_bytes=56 * MIB),
+            name="expand",
+        )(base.reshape(1), index, translators)
+
+    first = expand(0)
+    across_source, first, pattern = lax.optimization_barrier((across_source, first, pattern))
+    received = own, exchange(outgoing(across_source))
+    expanded = first, expand(1)
     pairs = jnp.where(far_mask == 1, tile_map, middle).reshape(-1)
-    lines = lines // 2
-    shape = (boxes * 2 * illum, unknowns)
-    neighbours = [[first * near + d for d in range(near)] for first in range(2)]
     steps = 4
 
     def translate(v):
@@ -283,21 +316,20 @@
                 grid=(half // steps,),
                 in_specs=[
                     pl.BlockSpec(block, lambda k, pairs: (0, 0, 0, 0, 0)),
+                    pl.BlockSpec(block, lambda k, pairs: (0, 0, 0, 0, 0)),
                     pl.BlockSpec(
-                        (1, 2, steps, count, columns, 2 * LANES), lambda k, pairs: (v, 0, k, 0, 0, 0)
+                        (1, steps, count, columns, 2 * LANES), lambda k, pairs: (v, k, 0, 0, 0)
                     ),
-                ],
-                out_specs=pl.BlockSpec((near,) + block[1:], lambda k, pairs: (0, 0, 0, 0, 0)),
+                    pl.BlockSpec(
+                        (1, steps, count, columns, 2 * LANES), lambda k, pairs: (v, k, 0, 0, 0)
+                    ),
+                ],
+                out_specs=pl.BlockSpec(block, lambda k, pairs: (0, 0, 0, 0, 0)),
             ),
-            out_shape=jax.ShapeDtypeStruct((near,) + block[1:], jnp.bfloat16),
+            out_shape=jax.ShapeDtypeStruct(block, jnp.bfloat16),
             compiler_params=pltpu.CompilerParams(vmem_limit_bytes=50 * MIB),
             name="translate",
-        )(pairs, received, expanded)
-
-    def exchange(values):
-        return lax.all_to_all(
-            values, OWNERS, split_axis=0, concat_axis=0, tiled=True, axis_index_groups=neighbours
-        )
+        )(pairs, *received, *expanded)
 
     def field(values, kind):
         return pl.pallas_call(
@@ -313,9 +345,7 @@
 
     far_half = exchange(translate(0))
     near_half = exchange(translate(1))
-    across = lax.ppermute(
-        field(far_half, jnp.bfloat16), "wide", [(w, (w + wide // 2) % wide) for w in range(wide)]
-    )
+    across = cross(field(far_half, jnp.bfloat16))
     total = field(near_half, jnp.float32) + across.astype(jnp.float32)
     return total.astype(jnp.bfloat16).reshape(source.shape)
 

time: 119 us -> 117 us (0.983)
  waiting for transfers between devices: 47.9 us -> 39.9 us
  Pallas kernels: 37 us -> 41.3 us
    all_to_all x1 -> x0, waiting for transfers between devices: 20.6 us -> none  [tiled_local(): lax.all_to_all(outgoing.reshape(block), OWNERS, split_axis=0, concat_axis...]
    all_to_all x1 -> x0, starting transfers between devices: 7.36 us -> none  [tiled_local(): lax.all_to_all(outgoing.reshape(block), OWNERS, split_axis=0, concat_axis...]
    all_to_all x2 -> x4, waiting for transfers between devices: 27.3 us -> 34.6 us  [exchange(): lax.all_to_all(values, OWNERS, split_axis=0, concat_axis=0, tiled=True, a...]
    ppermute x1 -> x2, waiting for transfers between devices: 0.01 us -> 5.32 us  [cross(): lax.ppermute(values, 'wide', [(w, (w + wide // 2) % wide) for w in range(...]
    all_to_all x2 -> x4, starting transfers between devices: 13.8 us -> 19 us  [exchange(): lax.all_to_all(values, OWNERS, split_axis=0, concat_axis=0, tiled=True, a...]
    pallas_call x2 -> x4, Pallas kernels: 16.6 us -> 21.1 us  [the longest x2 13.9 us: expand(): pl.pallas_call(functools.partial(expand_kernel, middle), grid_spec=pltpu....]
    ppermute x1 -> x2, starting transfers between devices: 2.65 us -> 5.33 us  [cross(): lax.ppermute(values, 'wide', [(w, (w + wide // 2) % wide) for w in range(...]
    unnamed x9 -> x11, local copies, waits for them, and re-layouts: 7.99 us -> 8.75 us
  transfers between devices with their start and end apart: 4 -> 6, of which waited for: 3 -> 4; matrix products, arithmetic and copies ran while one was open for 7% -> 8% of each run, Pallas kernels for 19% -> 25%
where the time goes in v2:
time: 117 us; the launch traced here: 116 us
  Pallas kernels  41.3 us (35%)
  waiting for transfers between devices  39.9 us (34%)
  starting transfers between devices  24.4 us (21%)
  local copies, waits for them, and re-layouts  8.91 us (8%)
  other arithmetic  1.68 us (1%)
    all_to_all x4, waiting for transfers between devices, exchange(): lax.all_to_all(values, OWNERS, split_axis=0, concat_axis=0, tiled=True, a...  34.6 us
    all_to_all x4, starting transfers between devices, exchange(): lax.all_to_all(values, OWNERS, split_axis=0, concat_axis=0, tiled=True, a...  19 us
    pallas_call x2, Pallas kernels, translate(): pl.pallas_call(functools.partial(translate_kernel, wide, slab, sub, rows,...  18.2 us
    pallas_call x2, Pallas kernels, expand(): pl.pallas_call(functools.partial(expand_kernel, middle), grid_spec=pltpu....  13.9 us
    unnamed x11, local copies, waits for them, and re-layouts  8.75 us
    pallas_call x2, Pallas kernels, outgoing(): pl.pallas_call(functools.partial(outgoing_kernel, boxes, illum, near, hal...  7.13 us
    ppermute x2, starting transfers between devices, cross(): lax.ppermute(values, 'wide', [(w, (w + wide // 2) % wide) for w in range(...  5.33 us
    ppermute x2, waiting for transfers between devices, cross(): lax.ppermute(values, 'wide', [(w, (w + wide // 2) % wide) for w in range(...  5.32 us
  transfers between devices with their start and end apart: 6, of which 4 were waited for; matrix products, arithmetic and copies ran while one was open for 8% of the time, Pallas kernels for 25%

profile of v2, /device:TPU:0, one launch (start us, length us, event | category | flops | bytes accessed | tf_op | source)
XLA Modules:
  0.0 116.3 jit_solution(6340520111973376498)
XLA Ops:
  0.0 3.6 %outgoing.2 = bf16[4096,128]{1,0:T(8,128)(2,1)} custom-call(s32[1]{0:T(128)} %bitcast.place_ref, bf16[2048,128]{1,0:T(8,128)(2,1)} %bitcast.17, bf16[2,512,128]{2,1,0:T(8,128)(2,1)} %agg_ref.3), custom_call_target="tpu_custom_call" | custom-call | tf_op jit(solution)/shard_map/outgoing/pallas_call | solution.py:230
  3.6 5.2 %all-to-all-start = ((bf16[8,16,2,16,128]{4,3,2,1,0:T(8,128)(2,1)}), bf16[8,16,2,16,128]{4,3,2,1,0:T(8,128)(2,1)S(1)}, u32[]{:S(2)}, u32[]{:S(2)}) async-start(bf16[8,16,2,16,128]{4,3,2,1,0:T(8,128)(2,1)} %bitcast.15), calls=%async_computation | async-start | bytes 2097152 | tf_op jit(solution)/shard_map/all_to_all | solution.py:222
  8.9 2.6 %collective-permute-start = (bf16[2048,128]{1,0:T(8,128)(2,1)}, bf16[2048,128]{1,0:T(8,128)(2,1)S(1)}, u32[]{:S(2)}, u32[]{:S(2)}) collective-permute-start(bf16[2048,128]{1,0:T(8,128)(2,1)} %bitcast.18), channel_id=1, source_target_pairs={{0,8},{4,12},{8,0},{12,4},{1,9},{5,13},{9,1},{13,5},{2,10},{6,14},... | collective-permute-start | bytes 1572872 | tf_op jit(solution)/shard_map/ppermute | solution.py:227
  11.4 7.9 %copy.11.table_ref = bf16[2,128,31,255]{3,2,1,0:T(8,128)(2,1)} copy(bf16[2,128,31,255]{1,0,3,2:T(2,128)(2,1)} %param.9) | data formatting | bytes 8094720 | tf_op args[2]
  19.4 0.1 pattern.1.pattern_ref
  19.6 0.1 copy_select_fusion
  19.7 0.7 pad_add_fusion.2.index_ref
  20.4 6.9 %expand.2.low_ref = bf16[2,16,31,16,256]{4,3,2,1,0:T(8,128)(2,1)} custom-call(s32[1]{0:T(128)} %bitcast.3.base_ref, s32[32,128]{1,0:T(8,128)} %pad_add_fusion.2.index_ref, bf16[2,128,31,255]{3,2,1,0:T(8,128)(2,1)} %copy.11.table_ref), custom_call_target="tpu_custom_call" | custom-call | tf_op jit(solution)/shard_map/expand/pallas_call | solution.py:278
  27.3 5.3 %collective-permute-done.src_ref = bf16[2048,128]{1,0:T(8,128)(2,1)S(1)} collective-permute-done((bf16[2048,128]{1,0:T(8,128)(2,1)}, bf16[2048,128]{1,0:T(8,128)(2,1)S(1)}, u32[]{:S(2)}, u32[]{:S(2)}) %collective-permute-start) | collective-permute-done | bytes 524320 | tf_op jit(solution)/shard_map/ppermute | solution.py:227
  32.6 0.8 copy-done.1
  33.4 3.5 %outgoing.3 = bf16[4096,128]{1,0:T(8,128)(2,1)} custom-call(s32[1]{0:T(128)} %bitcast.place_ref, bf16[2048,128]{1,0:T(8,128)(2,1)} %copy-done.1, bf16[2,512,128]{2,1,0:T(8,128)(2,1)} %agg_ref.3), custom_call_target="tpu_custom_call" | custom-call | tf_op jit(solution)/shard_map/outgoing/pallas_call | solution.py:230
  36.9 6.7 %all-to-all-start.1 = ((bf16[8,16,2,16,128]{4,3,2,1,0:T(8,128)(2,1)}), bf16[8,16,2,16,128]{4,3,2,1,0:T(8,128)(2,1)S(1)}, u32[]{:S(2)}, u32[]{:S(2)}) async-start(bf16[8,16,2,16,128]{4,3,2,1,0:T(8,128)(2,1)} %bitcast.16), calls=%async_computation.1 | async-start | bytes 2097152 | tf_op jit(solution)/shard_map/all_to_all | solution.py:222
  43.6 7.0 %expand.3.high_ref = bf16[2,16,31,16,256]{4,3,2,1,0:T(8,128)(2,1)} custom-call(s32[1]{0:T(128)} %bitcast.3.base_ref, s32[32,128]{1,0:T(8,128)} %pad_add_fusion.2.index_ref, bf16[2,128,31,255]{3,2,1,0:T(8,128)(2,1)} %copy.11.table_ref), custom_call_target="tpu_custom_call" | custom-call | tf_op jit(solution)/shard_map/expand/pallas_call | solution.py:278
  50.7 7.3 %all-to-all-done.1.far_ref = bf16[8,16,2,16,128]{4,3,2,1,0:T(8,128)(2,1)S(1)} async-done(((bf16[8,16,2,16,128]{4,3,2,1,0:T(8,128)(2,1)}), bf16[8,16,2,16,128]{4,3,2,1,0:T(8,128)(2,1)S(1)}, u32[]{:S(2)}, u32[]{:S(2)}) %all-to-all-start.1) | async-done | bytes 1048608 | tf_op jit(solution)/shard_map/all_to_all | solution.py:222
  58.1 9.1 %translate.3 = bf16[8,16,2,16,128]{4,3,2,1,0:T(8,128)(2,1)} custom-call(s32[64]{0:T(128)S(1)} %reshape.39.pair_ref, bf16[8,16,2,16,128]{4,3,2,1,0:T(8,128)(2,1)S(1)} %all-to-all-done.own_ref, bf16[8,16,2,16,128]{4,3,2,1,0:T(8,128)(2,1)S(1)} %all-to-all-done.1.far_ref, bf16[2,16,31,16,256]{4,3,2,1,0:T(8,128)(2,1)} %expand.2.low_ref, ...), custom_call_target="tpu_custom_call" | custom-call | tf_op jit(solution)/shard_map/translate/pallas_call | solution.py:312
  67.2 3.6 %all-to-all-start.3 = ((bf16[8,16,2,16,128]{4,3,2,1,0:T(8,128)(2,1)}), bf16[8,16,2,16,128]{4,3,2,1,0:T(8,128)(2,1)S(1)}, u32[]{:S(2)}, u32[]{:S(2)}) async-start(bf16[8,16,2,16,128]{4,3,2,1,0:T(8,128)(2,1)} %translate.3), calls=%async_computation.3 | async-start | bytes 2097152 | tf_op jit(solution)/shard_map/all_to_all | solution.py:222
  70.7 9.1 %translate.2 = bf16[8,16,2,16,128]{4,3,2,1,0:T(8,128)(2,1)} custom-call(s32[64]{0:T(128)S(1)} %reshape.39.pair_ref, bf16[8,16,2,16,128]{4,3,2,1,0:T(8,128)(2,1)S(1)} %all-to-all-done.own_ref, bf16[8,16,2,16,128]{4,3,2,1,0:T(8,128)(2,1)S(1)} %all-to-all-done.1.far_ref, bf16[2,16,31,16,256]{4,3,2,1,0:T(8,128)(2,1)} %expand.2.low_ref, ...), custom_call_target="tpu_custom_call" | custom-call | tf_op jit(solution)/shard_map/translate/pallas_call | solution.py:312
  79.8 5.3 %all-to-all-done.3 = bf16[8,16,2,16,128]{4,3,2,1,0:T(8,128)(2,1)S(1)} async-done(((bf16[8,16,2,16,128]{4,3,2,1,0:T(8,128)(2,1)}), bf16[8,16,2,16,128]{4,3,2,1,0:T(8,128)(2,1)S(1)}, u32[]{:S(2)}, u32[]{:S(2)}) %all-to-all-start.3) | async-done | bytes 1048608 | tf_op jit(solution)/shard_map/all_to_all | solution.py:222
  85.1 3.6 %all-to-all-start.2 = ((bf16[8,16,2,16,128]{4,3,2,1,0:T(8,128)(2,1)}), bf16[8,16,2,16,128]{4,3,2,1,0:T(8,128)(2,1)S(1)}, u32[]{:S(2)}, u32[]{:S(2)}) async-start(bf16[8,16,2,16,128]{4,3,2,1,0:T(8,128)(2,1)} %translate.2), calls=%async_computation.2 | async-start | bytes 2097152 | tf_op jit(solution)/shard_map/all_to_all | solution.py:222
  88.7 1.0 field.3
  89.7 2.7 %collective-permute-start.1 = (bf16[2048,128]{1,0:T(8,128)(2,1)S(1)}, bf16[2048,128]{1,0:T(8,128)(2,1)S(1)}, u32[]{:S(2)}, u32[]{:S(2)}) collective-permute-start(bf16[2048,128]{1,0:T(8,128)(2,1)S(1)} %field.3), channel_id=1, source_target_pairs={{0,8},{4,12},{8,0},{12,4},{1,9},{5,13},{9,1},{13,5},{2,10},{6,14},... | collective-permute-start | bytes 1572872 | tf_op jit(solution)/shard_map/ppermute | solution.py:227
  92.4 21.9 %all-to-all-done.2 = bf16[8,16,2,16,128]{4,3,2,1,0:T(8,128)(2,1)S(1)} async-done(((bf16[8,16,2,16,128]{4,3,2,1,0:T(8,128)(2,1)}), bf16[8,16,2,16,128]{4,3,2,1,0:T(8,128)(2,1)S(1)}, u32[]{:S(2)}, u32[]{:S(2)}) %all-to-all-start.2) | async-done | bytes 1048608 | tf_op jit(solution)/shard_map/all_to_all | solution.py:222
  114.3 1.0 field.2
  115.4 0.9 add_convert_fusion
  (17 shorter events, 0.2 us)
Async XLA Ops:
  0.0 19.4 %copy-start = (bf16[2,128,512]{2,1,0:T(8,128)(2,1)S(1)}, bf16[2,128,512]{2,1,0:T(8,128)(2,1)}, u32[]{:S(2)}) copy-start(bf16[2,128,512]{2,1,0:T(8,128)(2,1)} %dis_ref.1) | copy-start | bytes 786436
  0.0 19.5 %copy-start.2 = (s32[64,64]{1,0:T(8,128)S(1)}, s32[64,64]{1,0:T(8,128)}, u32[]{:S(2)}) copy-start(s32[64,64]{1,0:T(8,128)} %param.12) | copy-start | bytes 49156
  3.6 33.3 %all-to-all-start = ((bf16[8,16,2,16,128]{4,3,2,1,0:T(8,128)(2,1)}), bf16[8,16,2,16,128]{4,3,2,1,0:T(8,128)(2,1)S(1)}, u32[]{:S(2)}, u32[]{:S(2)}) async-start(bf16[8,16,2,16,128]{4,3,2,1,0:T(8,128)(2,1)} %bitcast.15), calls=%async_computation | async-start | bytes 2097152 | tf_op jit(solution)/shard_map/all_to_all | solution.py:222
  8.9 23.8 %collective-permute-start = (bf16[2048,128]{1,0:T(8,128)(2,1)}, bf16[2048,128]{1,0:T(8,128)(2,1)S(1)}, u32[]{:S(2)}, u32[]{:S(2)}) collective-permute-start(bf16[2048,128]{1,0:T(8,128)(2,1)} %bitcast.18), channel_id=1, source_target_pairs={{0,8},{4,12},{8,0},{12,4},{1,9},{5,13},{9,1},{13,5},{2,10},{6,14},... | collective-permute-start | bytes 1572872 | tf_op jit(solution)/shard_map/ppermute | solution.py:227
  27.3 23.3 %copy-start.3 = (s32[8,8]{1,0:T(8,128)S(1)}, s32[8,8]{1,0:T(8,128)}, u32[]{:S(2)}) copy-start(s32[8,8]{1,0:T(8,128)} %param.10) | copy-start | bytes 772
  27.3 23.3 %copy-start.4 = (s32[8,8]{1,0:T(8,128)S(1)}, s32[8,8]{1,0:T(8,128)}, u32[]{:S(2)}) copy-start(s32[8,8]{1,0:T(8,128)} %param.11) | copy-start | bytes 772
  32.6 0.8 copy-start.1
  36.9 21.2 %all-to-all-start.1 = ((bf16[8,16,2,16,128]{4,3,2,1,0:T(8,128)(2,1)}), bf16[8,16,2,16,128]{4,3,2,1,0:T(8,128)(2,1)S(1)}, u32[]{:S(2)}, u32[]{:S(2)}) async-start(bf16[8,16,2,16,128]{4,3,2,1,0:T(8,128)(2,1)} %bitcast.16), calls=%async_computation.1 | async-start | bytes 2097152 | tf_op jit(solution)/shard_map/all_to_all | solution.py:222
  67.2 17.9 %all-to-all-start.3 = ((bf16[8,16,2,16,128]{4,3,2,1,0:T(8,128)(2,1)}), bf16[8,16,2,16,128]{4,3,2,1,0:T(8,128)(2,1)S(1)}, u32[]{:S(2)}, u32[]{:S(2)}) async-start(bf16[8,16,2,16,128]{4,3,2,1,0:T(8,128)(2,1)} %translate.3), calls=%async_computation.3 | async-start | bytes 2097152 | tf_op jit(solution)/shard_map/all_to_all | solution.py:222
  85.1 29.2 %all-to-all-start.2 = ((bf16[8,16,2,16,128]{4,3,2,1,0:T(8,128)(2,1)}), bf16[8,16,2,16,128]{4,3,2,1,0:T(8,128)(2,1)S(1)}, u32[]{:S(2)}, u32[]{:S(2)}) async-start(bf16[8,16,2,16,128]{4,3,2,1,0:T(8,128)(2,1)} %translate.2), calls=%async_computation.2 | async-start | bytes 2097152 | tf_op jit(solution)/shard_map/all_to_all | solution.py:222
  89.7 25.7 %collective-permute-start.1 = (bf16[2048,128]{1,0:T(8,128)(2,1)S(1)}, bf16[2048,128]{1,0:T(8,128)(2,1)S(1)}, u32[]{:S(2)}, u32[]{:S(2)}) collective-permute-start(bf16[2048,128]{1,0:T(8,128)(2,1)S(1)} %field.3), channel_id=1, source_target_pairs={{0,8},{4,12},{8,0},{12,4},{1,9},{5,13},{9,1},{13,5},{2,10},{6,14},... | collective-permute-start | bytes 1572872 | tf_op jit(solution)/shard_map/ppermute | solution.py:227

commit v3 on v2

--- a/solution.py
+++ b/solution.py
@@ -226,7 +226,7 @@
     def cross(values):
         return lax.ppermute(values, "wide", [(w, (w + wide // 2) % wide) for w in range(wide)])
 
-    def outgoing(values):
+    def outgoing(values, limit):
         return pl.pallas_call(
             functools.partial(outgoing_kernel, boxes, illum, near, half),
             grid_spec=pltpu.PrefetchScalarGridSpec(
@@ -243,13 +243,13 @@
                 ],
             ),
             out_shape=jax.ShapeDtypeStruct((lines, LANES), jnp.bfloat16),
-            compiler_params=pltpu.CompilerParams(vmem_limit_bytes=56 * MIB),
+            compiler_params=pltpu.CompilerParams(vmem_limit_bytes=limit * MIB),
             name="outgoing",
         )(place.reshape(1), values, aggregation).reshape(block)
 
     flat = source.reshape(shape)
     across_source = cross(flat)
-    own = exchange(outgoing(flat))
+    own = exchange(outgoing(flat, 56))
 
     side = box_offsets.shape[0]
     x_half = side // 2
@@ -298,12 +298,17 @@
             ),
             out_shape=jax.ShapeDtypeStruct((2, half, count, columns, 2 * LANES), jnp.bfloat16),
             compiler_params=pltpu.CompilerParams(vmem_limit_bytes=56 * MIB),
+            cost_estimate=pl.CostEstimate(
+                flops=8 * 2 * 2 * half * x_half * 2 * LANES * x_half * LANES,
+                bytes_accessed=8 * 2 * half * count * columns * 2 * LANES * 2,
+                transcendentals=0,
+            ),
             name="expand",
         )(base.reshape(1), index, translators)
 
     first = expand(0)
     across_source, first, pattern = lax.optimization_barrier((across_source, first, pattern))
-    received = own, exchange(outgoing(across_source))
+    received = own, exchange(outgoing(across_source, 16))
     expanded = first, expand(1)
     pairs = jnp.where(far_mask == 1, tile_map, middle).reshape(-1)
     steps = 4

time: 117 us -> 114 us (0.974)
  starting transfers between devices: 24.4 us -> 19.2 us
  waiting for transfers between devices: 39.9 us -> 41.8 us
    all_to_all x4, waiting for transfers between devices: 34.6 us -> 39.4 us  [exchange(): lax.all_to_all(values, OWNERS, split_axis=0, concat_axis=0, tiled=True, a...]
    all_to_all x4, starting transfers between devices: 19 us -> 14.5 us  [exchange(): lax.all_to_all(values, OWNERS, split_axis=0, concat_axis=0, tiled=True, a...]
    ppermute x2, waiting for transfers between devices: 5.32 us -> 2.48 us  [cross(): lax.ppermute(values, 'wide', [(w, (w + wide // 2) % wide) for w in range(...]
    unnamed x11 -> x9, local copies, waits for them, and re-layouts: 8.75 us -> 7.98 us
  transfers between devices with their start and end apart: 6 -> 6, of which waited for: 4 -> 5; matrix products, arithmetic and copies ran while one was open for 8% -> 9% of each run, Pallas kernels for 25% -> 28%
where the time goes in v3:
time: 114 us; the launch traced here: 113 us
  waiting for transfers between devices  41.8 us (37%)
  Pallas kernels  40.4 us (35%)
  starting transfers between devices  19.2 us (17%)
  local copies, waits for them, and re-layouts  9.7 us (9%)
  other arithmetic  1.67 us (1%)
    all_to_all x4, waiting for transfers between devices, exchange(): lax.all_to_all(values, OWNERS, split_axis=0, concat_axis=0, tiled=True, a...  39.4 us
    pallas_call x2, Pallas kernels, translate(): pl.pallas_call(functools.partial(translate_kernel, wide, slab, sub, rows,...  18.1 us
    all_to_all x4, starting transfers between devices, exchange(): lax.all_to_all(values, OWNERS, split_axis=0, concat_axis=0, tiled=True, a...  14.5 us
    pallas_call x2, Pallas kernels, expand(): pl.pallas_call(functools.partial(expand_kernel, middle), grid_spec=pltpu....  14 us
    unnamed x9, local copies, waits for them, and re-layouts  7.98 us
    pallas_call x2, Pallas kernels, outgoing(): pl.pallas_call(functools.partial(outgoing_kernel, boxes, illum, near, hal...  6.07 us
    ppermute x2, starting transfers between devices, cross(): lax.ppermute(values, 'wide', [(w, (w + wide // 2) % wide) for w in range(...  4.75 us
    ppermute x2, waiting for transfers between devices, cross(): lax.ppermute(values, 'wide', [(w, (w + wide // 2) % wide) for w in range(...  2.48 us
  transfers between devices with their start and end apart: 6, of which 5 were waited for; matrix products, arithmetic and copies ran while one was open for 9% of the time, Pallas kernels for 28%

profile of v3, /device:TPU:0, one launch (start us, length us, event | category | flops | bytes accessed | tf_op | source)
XLA Modules:
  0.0 112.9 jit_solution(12494881014460335763)
XLA Ops:
  0.0 4.0 %collective-permute-start = (bf16[2048,128]{1,0:T(8,128)(2,1)}, bf16[2048,128]{1,0:T(8,128)(2,1)S(1)}, u32[]{:S(2)}, u32[]{:S(2)}) collective-permute-start(bf16[2048,128]{1,0:T(8,128)(2,1)} %bitcast.16), channel_id=1, source_target_pairs={{0,8},{4,12},{8,0},{12,4},{1,9},{5,13},{9,1},{13,5},{2,10},{6,14},... | collective-permute-start | bytes 1572872 | tf_op jit(solution)/shard_map/ppermute | solution.py:227
  4.0 3.6 %outgoing.2 = bf16[4096,128]{1,0:T(8,128)(2,1)} custom-call(s32[1]{0:T(128)} %bitcast.place_ref, bf16[2048,128]{1,0:T(8,128)(2,1)} %bitcast.17, bf16[2,512,128]{2,1,0:T(8,128)(2,1)} %agg_ref.3), custom_call_target="tpu_custom_call" | custom-call | tf_op jit(solution)/shard_map/outgoing/pallas_call | solution.py:230
  7.7 3.8 %all-to-all-start = ((bf16[8,16,2,16,128]{4,3,2,1,0:T(8,128)(2,1)}), bf16[8,16,2,16,128]{4,3,2,1,0:T(8,128)(2,1)S(1)}, u32[]{:S(2)}, u32[]{:S(2)}) async-start(bf16[8,16,2,16,128]{4,3,2,1,0:T(8,128)(2,1)} %bitcast.15), calls=%async_computation | async-start | bytes 2097152 | tf_op jit(solution)/shard_map/all_to_all | solution.py:222
  11.4 0.7 fusion.1
  12.2 0.9 fusion.2
  13.2 8.0 %copy.11.table_ref = bf16[2,128,31,255]{3,2,1,0:T(8,128)(2,1)} copy(bf16[2,128,31,255]{1,0,3,2:T(2,128)(2,1)} %param.9) | data formatting | bytes 8094720 | tf_op args[2]
  21.2 0.7 pad_add_fusion.2.index_ref
  21.8 7.0 %expand.2.low_ref = bf16[2,16,31,16,256]{4,3,2,1,0:T(8,128)(2,1)} custom-call(s32[1]{0:T(128)} %bitcast.3.base_ref, s32[32,128]{1,0:T(8,128)} %pad_add_fusion.2.index_ref, bf16[2,128,31,255]{3,2,1,0:T(8,128)(2,1)} %copy.11.table_ref), custom_call_target="tpu_custom_call" | custom-call | flops 17179869184 | bytes 65011712 | tf_op jit(solution)/shard_map/expand/pallas_call | solution.py:278
  29.0 2.4 %outgoing.3 = bf16[4096,128]{1,0:T(8,128)(2,1)} custom-call(s32[1]{0:T(128)} %bitcast.place_ref, bf16[2048,128]{1,0:T(8,128)(2,1)S(1)} %collective-permute-done.src_ref, bf16[2,512,128]{2,1,0:T(8,128)(2,1)S(1)} %copy-done), custom_call_target="tpu_custom_call" | custom-call | tf_op jit(solution)/shard_map/outgoing/pallas_call | solution.py:230
  31.5 4.5 %all-to-all-done.own_ref = bf16[8,16,2,16,128]{4,3,2,1,0:T(8,128)(2,1)S(1)} async-done(((bf16[8,16,2,16,128]{4,3,2,1,0:T(8,128)(2,1)}), bf16[8,16,2,16,128]{4,3,2,1,0:T(8,128)(2,1)S(1)}, u32[]{:S(2)}, u32[]{:S(2)}) %all-to-all-start) | async-done | bytes 1048608 | tf_op jit(solution)/shard_map/all_to_all | solution.py:222
  36.0 3.6 %all-to-all-start.1 = ((bf16[8,16,2,16,128]{4,3,2,1,0:T(8,128)(2,1)}), bf16[8,16,2,16,128]{4,3,2,1,0:T(8,128)(2,1)S(1)}, u32[]{:S(2)}, u32[]{:S(2)}) async-start(bf16[8,16,2,16,128]{4,3,2,1,0:T(8,128)(2,1)} %bitcast.9), calls=%async_computation.1 | async-start | bytes 2097152 | tf_op jit(solution)/shard_map/all_to_all | solution.py:222
  39.7 7.0 %expand.3.high_ref = bf16[2,16,31,16,256]{4,3,2,1,0:T(8,128)(2,1)} custom-call(s32[1]{0:T(128)} %bitcast.3.base_ref, s32[32,128]{1,0:T(8,128)} %pad_add_fusion.2.index_ref, bf16[2,128,31,255]{3,2,1,0:T(8,128)(2,1)} %copy.11.table_ref), custom_call_target="tpu_custom_call" | custom-call | flops 17179869184 | bytes 65011712 | tf_op jit(solution)/shard_map/expand/pallas_call | solution.py:278
  46.7 7.2 %all-to-all-done.1.far_ref = bf16[8,16,2,16,128]{4,3,2,1,0:T(8,128)(2,1)S(1)} async-done(((bf16[8,16,2,16,128]{4,3,2,1,0:T(8,128)(2,1)}), bf16[8,16,2,16,128]{4,3,2,1,0:T(8,128)(2,1)S(1)}, u32[]{:S(2)}, u32[]{:S(2)}) %all-to-all-start.1) | async-done | bytes 1048608 | tf_op jit(solution)/shard_map/all_to_all | solution.py:222
  53.9 9.1 %translate.3 = bf16[8,16,2,16,128]{4,3,2,1,0:T(8,128)(2,1)} custom-call(s32[64]{0:T(128)S(1)} %reshape.39.pair_ref, bf16[8,16,2,16,128]{4,3,2,1,0:T(8,128)(2,1)S(1)} %all-to-all-done.own_ref, bf16[8,16,2,16,128]{4,3,2,1,0:T(8,128)(2,1)S(1)} %all-to-all-done.1.far_ref, bf16[2,16,31,16,256]{4,3,2,1,0:T(8,128)(2,1)} %expand.2.low_ref, ...), custom_call_target="tpu_custom_call" | custom-call | tf_op jit(solution)/shard_map/translate/pallas_call | solution.py:317
  63.0 3.6 %all-to-all-start.3 = ((bf16[8,16,2,16,128]{4,3,2,1,0:T(8,128)(2,1)}), bf16[8,16,2,16,128]{4,3,2,1,0:T(8,128)(2,1)S(1)}, u32[]{:S(2)}, u32[]{:S(2)}) async-start(bf16[8,16,2,16,128]{4,3,2,1,0:T(8,128)(2,1)} %translate.3), calls=%async_computation.3 | async-start | bytes 2097152 | tf_op jit(solution)/shard_map/all_to_all | solution.py:222
  66.6 9.0 %translate.2 = bf16[8,16,2,16,128]{4,3,2,1,0:T(8,128)(2,1)} custom-call(s32[64]{0:T(128)S(1)} %reshape.39.pair_ref, bf16[8,16,2,16,128]{4,3,2,1,0:T(8,128)(2,1)S(1)} %all-to-all-done.own_ref, bf16[8,16,2,16,128]{4,3,2,1,0:T(8,128)(2,1)S(1)} %all-to-all-done.1.far_ref, bf16[2,16,31,16,256]{4,3,2,1,0:T(8,128)(2,1)} %expand.2.low_ref, ...), custom_call_target="tpu_custom_call" | custom-call | tf_op jit(solution)/shard_map/translate/pallas_call | solution.py:317
  75.6 5.3 %all-to-all-done.3 = bf16[8,16,2,16,128]{4,3,2,1,0:T(8,128)(2,1)S(1)} async-done(((bf16[8,16,2,16,128]{4,3,2,1,0:T(8,128)(2,1)}), bf16[8,16,2,16,128]{4,3,2,1,0:T(8,128)(2,1)S(1)}, u32[]{:S(2)}, u32[]{:S(2)}) %all-to-all-start.3) | async-done | bytes 1048608 | tf_op jit(solution)/shard_map/all_to_all | solution.py:222
  80.9 3.6 %all-to-all-start.2 = ((bf16[8,16,2,16,128]{4,3,2,1,0:T(8,128)(2,1)}), bf16[8,16,2,16,128]{4,3,2,1,0:T(8,128)(2,1)S(1)}, u32[]{:S(2)}, u32[]{:S(2)}) async-start(bf16[8,16,2,16,128]{4,3,2,1,0:T(8,128)(2,1)} %translate.2), calls=%async_computation.2 | async-start | bytes 2097152 | tf_op jit(solution)/shard_map/all_to_all | solution.py:222
  84.5 1.0 field.3
  85.5 0.7 collective-permute-start.1
  86.2 22.3 %all-to-all-done.2 = bf16[8,16,2,16,128]{4,3,2,1,0:T(8,128)(2,1)S(1)} async-done(((bf16[8,16,2,16,128]{4,3,2,1,0:T(8,128)(2,1)}), bf16[8,16,2,16,128]{4,3,2,1,0:T(8,128)(2,1)S(1)}, u32[]{:S(2)}, u32[]{:S(2)}) %all-to-all-start.2) | async-done | bytes 1048608 | tf_op jit(solution)/shard_map/all_to_all | solution.py:222
  108.4 1.0 field.2
  109.5 2.5 %collective-permute-done.1 = bf16[2048,128]{1,0:T(8,128)(2,1)S(1)} collective-permute-done((bf16[2048,128]{1,0:T(8,128)(2,1)S(1)}, bf16[2048,128]{1,0:T(8,128)(2,1)S(1)}, u32[]{:S(2)}, u32[]{:S(2)}) %collective-permute-start.1) | collective-permute-done | bytes 524320 | tf_op jit(solution)/shard_map/ppermute | solution.py:227
  112.0 0.9 add_convert_fusion
  (15 shorter events, 0.3 us)
Async XLA Ops:
  0.0 29.0 %collective-permute-start = (bf16[2048,128]{1,0:T(8,128)(2,1)}, bf16[2048,128]{1,0:T(8,128)(2,1)S(1)}, u32[]{:S(2)}, u32[]{:S(2)}) collective-permute-start(bf16[2048,128]{1,0:T(8,128)(2,1)} %bitcast.16), channel_id=1, source_target_pairs={{0,8},{4,12},{8,0},{12,4},{1,9},{5,13},{9,1},{13,5},{2,10},{6,14},... | collective-permute-start | bytes 1572872 | tf_op jit(solution)/shard_map/ppermute | solution.py:227
  7.7 28.3 %all-to-all-start = ((bf16[8,16,2,16,128]{4,3,2,1,0:T(8,128)(2,1)}), bf16[8,16,2,16,128]{4,3,2,1,0:T(8,128)(2,1)S(1)}, u32[]{:S(2)}, u32[]{:S(2)}) async-start(bf16[8,16,2,16,128]{4,3,2,1,0:T(8,128)(2,1)} %bitcast.15), calls=%async_computation | async-start | bytes 2097152 | tf_op jit(solution)/shard_map/all_to_all | solution.py:222
  21.8 7.0 %copy-start.1 = (bf16[2,128,512]{2,1,0:T(8,128)(2,1)S(1)}, bf16[2,128,512]{2,1,0:T(8,128)(2,1)}, u32[]{:S(2)}) copy-start(bf16[2,128,512]{2,1,0:T(8,128)(2,1)} %dis_ref.1) | copy-start | bytes 786436
  21.8 7.2 %copy-start = (bf16[2,512,128]{2,1,0:T(8,128)(2,1)S(1)}, bf16[2,512,128]{2,1,0:T(8,128)(2,1)}, u32[]{:S(2)}) copy-start(bf16[2,512,128]{2,1,0:T(8,128)(2,1)} %agg_ref.3) | copy-start | bytes 786436
  21.8 17.7 %copy-start.2 = (s32[8,8]{1,0:T(8,128)S(1)}, s32[8,8]{1,0:T(8,128)}, u32[]{:S(2)}) copy-start(s32[8,8]{1,0:T(8,128)} %param.10) | copy-start | bytes 772
  21.8 17.7 %copy-start.3 = (s32[8,8]{1,0:T(8,128)S(1)}, s32[8,8]{1,0:T(8,128)}, u32[]{:S(2)}) copy-start(s32[8,8]{1,0:T(8,128)} %param.11) | copy-start | bytes 772
  36.0 17.9 %all-to-all-start.1 = ((bf16[8,16,2,16,128]{4,3,2,1,0:T(8,128)(2,1)}), bf16[8,16,2,16,128]{4,3,2,1,0:T(8,128)(2,1)S(1)}, u32[]{:S(2)}, u32[]{:S(2)}) async-start(bf16[8,16,2,16,128]{4,3,2,1,0:T(8,128)(2,1)} %bitcast.9), calls=%async_computation.1 | async-start | bytes 2097152 | tf_op jit(solution)/shard_map/all_to_all | solution.py:222
  63.0 17.9 %all-to-all-start.3 = ((bf16[8,16,2,16,128]{4,3,2,1,0:T(8,128)(2,1)}), bf16[8,16,2,16,128]{4,3,2,1,0:T(8,128)(2,1)S(1)}, u32[]{:S(2)}, u32[]{:S(2)}) async-start(bf16[8,16,2,16,128]{4,3,2,1,0:T(8,128)(2,1)} %translate.3), calls=%async_computation.3 | async-start | bytes 2097152 | tf_op jit(solution)/shard_map/all_to_all | solution.py:222
  80.9 27.5 %all-to-all-start.2 = ((bf16[8,16,2,16,128]{4,3,2,1,0:T(8,128)(2,1)}), bf16[8,16,2,16,128]{4,3,2,1,0:T(8,128)(2,1)S(1)}, u32[]{:S(2)}, u32[]{:S(2)}) async-start(bf16[8,16,2,16,128]{4,3,2,1,0:T(8,128)(2,1)} %translate.2), calls=%async_computation.2 | async-start | bytes 2097152 | tf_op jit(solution)/shard_map/all_to_all | solution.py:222
  85.5 26.5 %collective-permute-start.1 = (bf16[2048,128]{1,0:T(8,128)(2,1)S(1)}, bf16[2048,128]{1,0:T(8,128)(2,1)S(1)}, u32[]{:S(2)}, u32[]{:S(2)}) collective-permute-start(bf16[2048,128]{1,0:T(8,128)(2,1)S(1)} %field.3), channel_id=1, source_target_pairs={{0,8},{4,12},{8,0},{12,4},{1,9},{5,13},{9,1},{13,5},{2,10},{6,14},... | collective-permute-start | bytes 1572872 | tf_op jit(solution)/shard_map/ppermute | solution.py:227

commit v4 on v3

--- a/solution.py
+++ b/solution.py
@@ -11,13 +11,14 @@
 LANES = 128
 MIB = 1024 * 1024
 PITCH = 36
+SPARE = 40
 NT = (((1,), (1,)), ((), ()))
 TN = (((0,), (0,)), ((), ()))
 
 
 def outgoing_kernel(boxes, illum, devices, half, place_ref, src_ref, agg_ref, out_ref, wide_src, wide_out):
     unknowns = src_ref.shape[1]
-    wide_src[...] = src_ref[...].astype(jnp.float32)
+    wide_src[0:src_ref.shape[0]] = src_ref[...].astype(jnp.float32)
     real = agg_ref[0].astype(jnp.float32)
     imag = agg_ref[1].astype(jnp.float32)
 
@@ -238,8 +239,8 @@
                 ],
                 out_specs=pl.BlockSpec((lines, LANES), lambda i, place: (0, 0)),
                 scratch_shapes=[
-                    pltpu.VMEM(shape, jnp.float32),
-                    pltpu.VMEM((near * half * PITCH, LANES), jnp.float32),
+                    pltpu.VMEM((shape[0] + SPARE, unknowns), jnp.float32),
+                    pltpu.VMEM((near * half * PITCH + SPARE, LANES), jnp.float32),
                 ],
             ),
             out_shape=jax.ShapeDtypeStruct((lines, LANES), jnp.bfloat16),
@@ -293,7 +294,7 @@
                 scratch_shapes=[
                     pltpu.VMEM((2 * LANES, x_half * LANES), jnp.bfloat16),
                     pltpu.VMEM((2 * batch * x_half, 2 * LANES), jnp.bfloat16),
-                    pltpu.VMEM((2 * batch * x_half * PITCH, LANES), jnp.float32),
+                    pltpu.VMEM((2 * batch * x_half * PITCH + SPARE, LANES), jnp.float32),
                 ],
             ),
             out_shape=jax.ShapeDtypeStruct((2, half, count, columns, 2 * LANES), jnp.bfloat16),
@@ -341,8 +342,8 @@
             functools.partial(field_kernel, boxes, illum),
             out_shape=jax.ShapeDtypeStruct(shape, kind),
             scratch_shapes=[
-                pltpu.VMEM((near * half * PITCH, LANES), jnp.float32),
-                pltpu.VMEM((boxes * PITCH, unknowns), jnp.float32),
+                pltpu.VMEM((near * half * PITCH + SPARE, LANES), jnp.float32),
+                pltpu.VMEM((boxes * PITCH + SPARE, unknowns), jnp.float32),
             ],
             compiler_params=pltpu.CompilerParams(vmem_limit_bytes=12 * MIB),
             name="field",

time: 114 us -> 114 us (level)
  no operation moved by 1% of the time
where the time goes in v4:
time: 114 us; the launch traced here: 113 us
  waiting for transfers between devices  41.8 us (37%)
  Pallas kernels  40.3 us (35%)
  starting transfers between devices  19.2 us (17%)
  local copies, waits for them, and re-layouts  9.7 us (9%)
  other arithmetic  1.67 us (1%)
    all_to_all x4, waiting for transfers between devices, exchange(): lax.all_to_all(values, OWNERS, split_axis=0, concat_axis=0, tiled=True, a...  39.4 us
    pallas_call x2, Pallas kernels, translate(): pl.pallas_call(functools.partial(translate_kernel, wide, slab, sub, rows,...  18.1 us
    all_to_all x4, starting transfers between devices, exchange(): lax.all_to_all(values, OWNERS, split_axis=0, concat_axis=0, tiled=True, a...  14.4 us
    pallas_call x2, Pallas kernels, expand(): pl.pallas_call(functools.partial(expand_kernel, middle), grid_spec=pltpu....  14 us
    unnamed x9, local copies, waits for them, and re-layouts  7.98 us
    pallas_call x2, Pallas kernels, outgoing(): pl.pallas_call(functools.partial(outgoing_kernel, boxes, illum, near, hal...  6.07 us
    ppermute x2, starting transfers between devices, cross(): lax.ppermute(values, 'wide', [(w, (w + wide // 2) % wide) for w in range(...  4.76 us
    ppermute x2, waiting for transfers between devices, cross(): lax.ppermute(values, 'wide', [(w, (w + wide // 2) % wide) for w in range(...  2.49 us
  transfers between devices with their start and end apart: 6, of which 5 were waited for; matrix products, arithmetic and copies ran while one was open for 9% of the time, Pallas kernels for 28%

profile of v4, /device:TPU:0, one launch (start us, length us, event | category | flops | bytes accessed | tf_op | source)
XLA Modules:
  0.0 112.9 jit_solution(17721336316855577707)
XLA Ops:
  0.0 4.0 %collective-permute-start = (bf16[2048,128]{1,0:T(8,128)(2,1)}, bf16[2048,128]{1,0:T(8,128)(2,1)S(1)}, u32[]{:S(2)}, u32[]{:S(2)}) collective-permute-start(bf16[2048,128]{1,0:T(8,128)(2,1)} %bitcast.16), channel_id=1, source_target_pairs={{0,8},{4,12},{8,0},{12,4},{1,9},{5,13},{9,1},{13,5},{2,10},{6,14},... | collective-permute-start | bytes 1572872 | tf_op jit(solution)/shard_map/ppermute | solution.py:228
  4.0 3.6 %outgoing.2 = bf16[4096,128]{1,0:T(8,128)(2,1)} custom-call(s32[1]{0:T(128)} %bitcast.place_ref, bf16[2048,128]{1,0:T(8,128)(2,1)} %bitcast.17, bf16[2,512,128]{2,1,0:T(8,128)(2,1)} %agg_ref.3), custom_call_target="tpu_custom_call" | custom-call | tf_op jit(solution)/shard_map/outgoing/pallas_call | solution.py:231
  7.7 3.8 %all-to-all-start = ((bf16[8,16,2,16,128]{4,3,2,1,0:T(8,128)(2,1)}), bf16[8,16,2,16,128]{4,3,2,1,0:T(8,128)(2,1)S(1)}, u32[]{:S(2)}, u32[]{:S(2)}) async-start(bf16[8,16,2,16,128]{4,3,2,1,0:T(8,128)(2,1)} %bitcast.15), calls=%async_computation | async-start | bytes 2097152 | tf_op jit(solution)/shard_map/all_to_all | solution.py:223
  11.4 0.7 fusion.1
  12.2 0.9 fusion.2
  13.2 8.0 %copy.11.table_ref = bf16[2,128,31,255]{3,2,1,0:T(8,128)(2,1)} copy(bf16[2,128,31,255]{1,0,3,2:T(2,128)(2,1)} %param.9) | data formatting | bytes 8094720 | tf_op args[2]
  21.1 0.7 pad_add_fusion.2.index_ref
  21.8 7.0 %expand.2.low_ref = bf16[2,16,31,16,256]{4,3,2,1,0:T(8,128)(2,1)} custom-call(s32[1]{0:T(128)} %bitcast.3.base_ref, s32[32,128]{1,0:T(8,128)} %pad_add_fusion.2.index_ref, bf16[2,128,31,255]{3,2,1,0:T(8,128)(2,1)} %copy.11.table_ref), custom_call_target="tpu_custom_call" | custom-call | flops 17179869184 | bytes 65011712 | tf_op jit(solution)/shard_map/expand/pallas_call | solution.py:279
  29.0 2.4 %outgoing.3 = bf16[4096,128]{1,0:T(8,128)(2,1)} custom-call(s32[1]{0:T(128)} %bitcast.place_ref, bf16[2048,128]{1,0:T(8,128)(2,1)S(1)} %collective-permute-done.src_ref, bf16[2,512,128]{2,1,0:T(8,128)(2,1)S(1)} %copy-done), custom_call_target="tpu_custom_call" | custom-call | tf_op jit(solution)/shard_map/outgoing/pallas_call | solution.py:231
  31.4 4.5 %all-to-all-done.own_ref = bf16[8,16,2,16,128]{4,3,2,1,0:T(8,128)(2,1)S(1)} async-done(((bf16[8,16,2,16,128]{4,3,2,1,0:T(8,128)(2,1)}), bf16[8,16,2,16,128]{4,3,2,1,0:T(8,128)(2,1)S(1)}, u32[]{:S(2)}, u32[]{:S(2)}) %all-to-all-start) | async-done | bytes 1048608 | tf_op jit(solution)/shard_map/all_to_all | solution.py:223
  36.0 3.6 %all-to-all-start.1 = ((bf16[8,16,2,16,128]{4,3,2,1,0:T(8,128)(2,1)}), bf16[8,16,2,16,128]{4,3,2,1,0:T(8,128)(2,1)S(1)}, u32[]{:S(2)}, u32[]{:S(2)}) async-start(bf16[8,16,2,16,128]{4,3,2,1,0:T(8,128)(2,1)} %bitcast.9), calls=%async_computation.1 | async-start | bytes 2097152 | tf_op jit(solution)/shard_map/all_to_all | solution.py:223
  39.6 7.0 %expand.3.high_ref = bf16[2,16,31,16,256]{4,3,2,1,0:T(8,128)(2,1)} custom-call(s32[1]{0:T(128)} %bitcast.3.base_ref, s32[32,128]{1,0:T(8,128)} %pad_add_fusion.2.index_ref, bf16[2,128,31,255]{3,2,1,0:T(8,128)(2,1)} %copy.11.table_ref), custom_call_target="tpu_custom_call" | custom-call | flops 17179869184 | bytes 65011712 | tf_op jit(solution)/shard_map/expand/pallas_call | solution.py:279
  46.7 7.2 %all-to-all-done.1.far_ref = bf16[8,16,2,16,128]{4,3,2,1,0:T(8,128)(2,1)S(1)} async-done(((bf16[8,16,2,16,128]{4,3,2,1,0:T(8,128)(2,1)}), bf16[8,16,2,16,128]{4,3,2,1,0:T(8,128)(2,1)S(1)}, u32[]{:S(2)}, u32[]{:S(2)}) %all-to-all-start.1) | async-done | bytes 1048608 | tf_op jit(solution)/shard_map/all_to_all | solution.py:223
  53.9 9.1 %translate.3 = bf16[8,16,2,16,128]{4,3,2,1,0:T(8,128)(2,1)} custom-call(s32[64]{0:T(128)S(1)} %reshape.39.pair_ref, bf16[8,16,2,16,128]{4,3,2,1,0:T(8,128)(2,1)S(1)} %all-to-all-done.own_ref, bf16[8,16,2,16,128]{4,3,2,1,0:T(8,128)(2,1)S(1)} %all-to-all-done.1.far_ref, bf16[2,16,31,16,256]{4,3,2,1,0:T(8,128)(2,1)} %expand.2.low_ref, ...), custom_call_target="tpu_custom_call" | custom-call | tf_op jit(solution)/shard_map/translate/pallas_call | solution.py:318
  63.0 3.6 %all-to-all-start.3 = ((bf16[8,16,2,16,128]{4,3,2,1,0:T(8,128)(2,1)}), bf16[8,16,2,16,128]{4,3,2,1,0:T(8,128)(2,1)S(1)}, u32[]{:S(2)}, u32[]{:S(2)}) async-start(bf16[8,16,2,16,128]{4,3,2,1,0:T(8,128)(2,1)} %translate.3), calls=%async_computation.3 | async-start | bytes 2097152 | tf_op jit(solution)/shard_map/all_to_all | solution.py:223
  66.5 9.1 %translate.2 = bf16[8,16,2,16,128]{4,3,2,1,0:T(8,128)(2,1)} custom-call(s32[64]{0:T(128)S(1)} %reshape.39.pair_ref, bf16[8,16,2,16,128]{4,3,2,1,0:T(8,128)(2,1)S(1)} %all-to-all-done.own_ref, bf16[8,16,2,16,128]{4,3,2,1,0:T(8,128)(2,1)S(1)} %all-to-all-done.1.far_ref, bf16[2,16,31,16,256]{4,3,2,1,0:T(8,128)(2,1)} %expand.2.low_ref, ...), custom_call_target="tpu_custom_call" | custom-call | tf_op jit(solution)/shard_map/translate/pallas_call | solution.py:318
  75.6 5.3 %all-to-all-done.3 = bf16[8,16,2,16,128]{4,3,2,1,0:T(8,128)(2,1)S(1)} async-done(((bf16[8,16,2,16,128]{4,3,2,1,0:T(8,128)(2,1)}), bf16[8,16,2,16,128]{4,3,2,1,0:T(8,128)(2,1)S(1)}, u32[]{:S(2)}, u32[]{:S(2)}) %all-to-all-start.3) | async-done | bytes 1048608 | tf_op jit(solution)/shard_map/all_to_all | solution.py:223
  80.9 3.6 %all-to-all-start.2 = ((bf16[8,16,2,16,128]{4,3,2,1,0:T(8,128)(2,1)}), bf16[8,16,2,16,128]{4,3,2,1,0:T(8,128)(2,1)S(1)}, u32[]{:S(2)}, u32[]{:S(2)}) async-start(bf16[8,16,2,16,128]{4,3,2,1,0:T(8,128)(2,1)} %translate.2), calls=%async_computation.2 | async-start | bytes 2097152 | tf_op jit(solution)/shard_map/all_to_all | solution.py:223
  84.5 1.0 field.3
  85.5 0.7 collective-permute-start.1
  86.2 22.3 %all-to-all-done.2 = bf16[8,16,2,16,128]{4,3,2,1,0:T(8,128)(2,1)S(1)} async-done(((bf16[8,16,2,16,128]{4,3,2,1,0:T(8,128)(2,1)}), bf16[8,16,2,16,128]{4,3,2,1,0:T(8,128)(2,1)S(1)}, u32[]{:S(2)}, u32[]{:S(2)}) %all-to-all-start.2) | async-done | bytes 1048608 | tf_op jit(solution)/shard_map/all_to_all | solution.py:223
  108.4 1.0 field.2
  109.5 2.5 %collective-permute-done.1 = bf16[2048,128]{1,0:T(8,128)(2,1)S(1)} collective-permute-done((bf16[2048,128]{1,0:T(8,128)(2,1)S(1)}, bf16[2048,128]{1,0:T(8,128)(2,1)S(1)}, u32[]{:S(2)}, u32[]{:S(2)}) %collective-permute-start.1) | collective-permute-done | bytes 524320 | tf_op jit(solution)/shard_map/ppermute | solution.py:228
  112.0 0.9 add_convert_fusion
  (15 shorter events, 0.3 us)
Async XLA Ops:
  0.0 29.0 %collective-permute-start = (bf16[2048,128]{1,0:T(8,128)(2,1)}, bf16[2048,128]{1,0:T(8,128)(2,1)S(1)}, u32[]{:S(2)}, u32[]{:S(2)}) collective-permute-start(bf16[2048,128]{1,0:T(8,128)(2,1)} %bitcast.16), channel_id=1, source_target_pairs={{0,8},{4,12},{8,0},{12,4},{1,9},{5,13},{9,1},{13,5},{2,10},{6,14},... | collective-permute-start | bytes 1572872 | tf_op jit(solution)/shard_map/ppermute | solution.py:228
  7.7 28.3 %all-to-all-start = ((bf16[8,16,2,16,128]{4,3,2,1,0:T(8,128)(2,1)}), bf16[8,16,2,16,128]{4,3,2,1,0:T(8,128)(2,1)S(1)}, u32[]{:S(2)}, u32[]{:S(2)}) async-start(bf16[8,16,2,16,128]{4,3,2,1,0:T(8,128)(2,1)} %bitcast.15), calls=%async_computation | async-start | bytes 2097152 | tf_op jit(solution)/shard_map/all_to_all | solution.py:223
  21.8 7.0 %copy-start.1 = (bf16[2,128,512]{2,1,0:T(8,128)(2,1)S(1)}, bf16[2,128,512]{2,1,0:T(8,128)(2,1)}, u32[]{:S(2)}) copy-start(bf16[2,128,512]{2,1,0:T(8,128)(2,1)} %dis_ref.1) | copy-start | bytes 786436
  21.8 7.2 %copy-start = (bf16[2,512,128]{2,1,0:T(8,128)(2,1)S(1)}, bf16[2,512,128]{2,1,0:T(8,128)(2,1)}, u32[]{:S(2)}) copy-start(bf16[2,512,128]{2,1,0:T(8,128)(2,1)} %agg_ref.3) | copy-start | bytes 786436
  21.8 17.7 %copy-start.2 = (s32[8,8]{1,0:T(8,128)S(1)}, s32[8,8]{1,0:T(8,128)}, u32[]{:S(2)}) copy-start(s32[8,8]{1,0:T(8,128)} %param.10) | copy-start | bytes 772
  21.8 17.7 %copy-start.3 = (s32[8,8]{1,0:T(8,128)S(1)}, s32[8,8]{1,0:T(8,128)}, u32[]{:S(2)}) copy-start(s32[8,8]{1,0:T(8,128)} %param.11) | copy-start | bytes 772
  36.0 17.9 %all-to-all-start.1 = ((bf16[8,16,2,16,128]{4,3,2,1,0:T(8,128)(2,1)}), bf16[8,16,2,16,128]{4,3,2,1,0:T(8,128)(2,1)S(1)}, u32[]{:S(2)}, u32[]{:S(2)}) async-start(bf16[8,16,2,16,128]{4,3,2,1,0:T(8,128)(2,1)} %bitcast.9), calls=%async_computation.1 | async-start | bytes 2097152 | tf_op jit(solution)/shard_map/all_to_all | solution.py:223
  63.0 17.9 %all-to-all-start.3 = ((bf16[8,16,2,16,128]{4,3,2,1,0:T(8,128)(2,1)}), bf16[8,16,2,16,128]{4,3,2,1,0:T(8,128)(2,1)S(1)}, u32[]{:S(2)}, u32[]{:S(2)}) async-start(bf16[8,16,2,16,128]{4,3,2,1,0:T(8,128)(2,1)} %translate.3), calls=%async_computation.3 | async-start | bytes 2097152 | tf_op jit(solution)/shard_map/all_to_all | solution.py:223
  80.9 27.5 %all-to-all-start.2 = ((bf16[8,16,2,16,128]{4,3,2,1,0:T(8,128)(2,1)}), bf16[8,16,2,16,128]{4,3,2,1,0:T(8,128)(2,1)S(1)}, u32[]{:S(2)}, u32[]{:S(2)}) async-start(bf16[8,16,2,16,128]{4,3,2,1,0:T(8,128)(2,1)} %translate.2), calls=%async_computation.2 | async-start | bytes 2097152 | tf_op jit(solution)/shard_map/all_to_all | solution.py:223
  85.5 26.5 %collective-permute-start.1 = (bf16[2048,128]{1,0:T(8,128)(2,1)S(1)}, bf16[2048,128]{1,0:T(8,128)(2,1)S(1)}, u32[]{:S(2)}, u32[]{:S(2)}) collective-permute-start(bf16[2048,128]{1,0:T(8,128)(2,1)S(1)} %field.3), channel_id=1, source_target_pairs={{0,8},{4,12},{8,0},{12,4},{1,9},{5,13},{9,1},{13,5},{2,10},{6,14},... | collective-permute-start | bytes 1572872 | tf_op jit(solution)/shard_map/ppermute | solution.py:228

commit v5 on v4

--- a/solution.py
+++ b/solution.py
@@ -99,7 +99,7 @@
     lower = lane < LANES // 2
     zero = jnp.zeros((illum, LANES), jnp.bfloat16)
     for step in range(steps):
-        here = pl.program_id(0) * steps + step
+        here = step
         sums = [None, None]
         turned = {}
 
@@ -272,7 +272,7 @@
         name="pattern",
     )(place.reshape(1), disaggregation)
     base = lax.axis_index("slab") * sub + lax.axis_index("sub")
-    batch = 4
+    batch = 8
 
     def expand(k2):
         per_part = half // batch
@@ -313,6 +313,7 @@
     expanded = first, expand(1)
     pairs = jnp.where(far_mask == 1, tile_map, middle).reshape(-1)
     steps = 4
+    part = (near, steps) + block[2:]
 
     def translate(v):
         return pl.pallas_call(
@@ -321,8 +322,8 @@
                 num_scalar_prefetch=1,
                 grid=(half // steps,),
                 in_specs=[
-                    pl.BlockSpec(block, lambda k, pairs: (0, 0, 0, 0, 0)),
-                    pl.BlockSpec(block, lambda k, pairs: (0, 0, 0, 0, 0)),
+                    pl.BlockSpec(part, lambda k, pairs: (0, k, 0, 0, 0)),
+                    pl.BlockSpec(part, lambda k, pairs: (0, k, 0, 0, 0)),
                     pl.BlockSpec(
                         (1, steps, count, columns, 2 * LANES), lambda k, pairs: (v, k, 0, 0, 0)
                     ),
@@ -330,7 +331,7 @@
                         (1, steps, count, columns, 2 * LANES), lambda k, pairs: (v, k, 0, 0, 0)
                     ),
                 ],
-                out_specs=pl.BlockSpec(block, lambda k, pairs: (0, 0, 0, 0, 0)),
+                out_specs=pl.BlockSpec(part, lambda k, pairs: (0, k, 0, 0, 0)),
             ),
             out_shape=jax.ShapeDtypeStruct(block, jnp.bfloat16),
             compiler_params=pltpu.CompilerParams(vmem_limit_bytes=50 * MIB),

time: 114 us -> 114 us (level)
  no operation moved by 1% of the time
where the time goes in v5:
time: 114 us; the launch traced here: 113 us
  waiting for transfers between devices  42.1 us (37%)
  Pallas kernels  40 us (35%)
  starting transfers between devices  19.2 us (17%)
  local copies, waits for them, and re-layouts  9.7 us (9%)
  other arithmetic  1.67 us (1%)
    all_to_all x4, waiting for transfers between devices, exchange(): lax.all_to_all(values, OWNERS, split_axis=0, concat_axis=0, tiled=True, a...  39.6 us
    pallas_call x2, Pallas kernels, translate(): pl.pallas_call(functools.partial(translate_kernel, wide, slab, sub, rows,...  17.9 us
    all_to_all x4, starting transfers between devices, exchange(): lax.all_to_all(values, OWNERS, split_axis=0, concat_axis=0, tiled=True, a...  14.4 us
    pallas_call x2, Pallas kernels, expand(): pl.pallas_call(functools.partial(expand_kernel, middle), grid_spec=pltpu....  13.9 us
    unnamed x9, local copies, waits for them, and re-layouts  7.98 us
    pallas_call x2, Pallas kernels, outgoing(): pl.pallas_call(functools.partial(outgoing_kernel, boxes, illum, near, hal...  6.07 us
    ppermute x2, starting transfers between devices, cross(): lax.ppermute(values, 'wide', [(w, (w + wide // 2) % wide) for w in range(...  4.75 us
    ppermute x2, waiting for transfers between devices, cross(): lax.ppermute(values, 'wide', [(w, (w + wide // 2) % wide) for w in range(...  2.5 us
  transfers between devices with their start and end apart: 6, of which 5 were waited for; matrix products, arithmetic and copies ran while one was open for 9% of the time, Pallas kernels for 28%

profile of v5, /device:TPU:0, one launch (start us, length us, event | category | flops | bytes accessed | tf_op | source)
XLA Modules:
  0.0 112.7 jit_solution(18256716057618710828)
XLA Ops:
  0.0 4.0 %collective-permute-start = (bf16[2048,128]{1,0:T(8,128)(2,1)}, bf16[2048,128]{1,0:T(8,128)(2,1)S(1)}, u32[]{:S(2)}, u32[]{:S(2)}) collective-permute-start(bf16[2048,128]{1,0:T(8,128)(2,1)} %bitcast.16), channel_id=1, source_target_pairs={{0,8},{4,12},{8,0},{12,4},{1,9},{5,13},{9,1},{13,5},{2,10},{6,14},... | collective-permute-start | bytes 1572872 | tf_op jit(solution)/shard_map/ppermute | solution.py:228
  4.0 3.6 %outgoing.2 = bf16[4096,128]{1,0:T(8,128)(2,1)} custom-call(s32[1]{0:T(128)} %bitcast.place_ref, bf16[2048,128]{1,0:T(8,128)(2,1)} %bitcast.17, bf16[2,512,128]{2,1,0:T(8,128)(2,1)} %agg_ref.3), custom_call_target="tpu_custom_call" | custom-call | tf_op jit(solution)/shard_map/outgoing/pallas_call | solution.py:231
  7.7 3.8 %all-to-all-start = ((bf16[8,16,2,16,128]{4,3,2,1,0:T(8,128)(2,1)}), bf16[8,16,2,16,128]{4,3,2,1,0:T(8,128)(2,1)S(1)}, u32[]{:S(2)}, u32[]{:S(2)}) async-start(bf16[8,16,2,16,128]{4,3,2,1,0:T(8,128)(2,1)} %bitcast.15), calls=%async_computation | async-start | bytes 2097152 | tf_op jit(solution)/shard_map/all_to_all | solution.py:223
  11.4 0.7 fusion.1
  12.2 0.9 fusion.2
  13.2 8.0 %copy.11.table_ref = bf16[2,128,31,255]{3,2,1,0:T(8,128)(2,1)} copy(bf16[2,128,31,255]{1,0,3,2:T(2,128)(2,1)} %param.9) | data formatting | bytes 8094720 | tf_op args[2]
  21.1 0.7 pad_add_fusion.2.index_ref
  21.8 7.0 %expand.2.low_ref = bf16[2,16,31,16,256]{4,3,2,1,0:T(8,128)(2,1)} custom-call(s32[1]{0:T(128)} %bitcast.3.base_ref, s32[32,128]{1,0:T(8,128)} %pad_add_fusion.2.index_ref, bf16[2,128,31,255]{3,2,1,0:T(8,128)(2,1)} %copy.11.table_ref), custom_call_target="tpu_custom_call" | custom-call | flops 17179869184 | bytes 65011712 | tf_op jit(solution)/shard_map/expand/pallas_call | solution.py:279
  29.0 2.4 %outgoing.3 = bf16[4096,128]{1,0:T(8,128)(2,1)} custom-call(s32[1]{0:T(128)} %bitcast.place_ref, bf16[2048,128]{1,0:T(8,128)(2,1)S(1)} %collective-permute-done.src_ref, bf16[2,512,128]{2,1,0:T(8,128)(2,1)S(1)} %copy-done), custom_call_target="tpu_custom_call" | custom-call | tf_op jit(solution)/shard_map/outgoing/pallas_call | solution.py:231
  31.4 4.6 %all-to-all-done.own_ref = bf16[8,16,2,16,128]{4,3,2,1,0:T(8,128)(2,1)S(1)} async-done(((bf16[8,16,2,16,128]{4,3,2,1,0:T(8,128)(2,1)}), bf16[8,16,2,16,128]{4,3,2,1,0:T(8,128)(2,1)S(1)}, u32[]{:S(2)}, u32[]{:S(2)}) %all-to-all-start) | async-done | bytes 1048608 | tf_op jit(solution)/shard_map/all_to_all | solution.py:223
  36.0 3.6 %all-to-all-start.1 = ((bf16[8,16,2,16,128]{4,3,2,1,0:T(8,128)(2,1)}), bf16[8,16,2,16,128]{4,3,2,1,0:T(8,128)(2,1)S(1)}, u32[]{:S(2)}, u32[]{:S(2)}) async-start(bf16[8,16,2,16,128]{4,3,2,1,0:T(8,128)(2,1)} %bitcast.9), calls=%async_computation.1 | async-start | bytes 2097152 | tf_op jit(solution)/shard_map/all_to_all | solution.py:223
  39.6 6.9 %expand.3.high_ref = bf16[2,16,31,16,256]{4,3,2,1,0:T(8,128)(2,1)} custom-call(s32[1]{0:T(128)} %bitcast.3.base_ref, s32[32,128]{1,0:T(8,128)} %pad_add_fusion.2.index_ref, bf16[2,128,31,255]{3,2,1,0:T(8,128)(2,1)} %copy.11.table_ref), custom_call_target="tpu_custom_call" | custom-call | flops 17179869184 | bytes 65011712 | tf_op jit(solution)/shard_map/expand/pallas_call | solution.py:279
  46.5 7.4 %all-to-all-done.1.far_ref = bf16[8,16,2,16,128]{4,3,2,1,0:T(8,128)(2,1)S(1)} async-done(((bf16[8,16,2,16,128]{4,3,2,1,0:T(8,128)(2,1)}), bf16[8,16,2,16,128]{4,3,2,1,0:T(8,128)(2,1)S(1)}, u32[]{:S(2)}, u32[]{:S(2)}) %all-to-all-start.1) | async-done | bytes 1048608 | tf_op jit(solution)/shard_map/all_to_all | solution.py:223
  53.9 9.0 %translate.3 = bf16[8,16,2,16,128]{4,3,2,1,0:T(8,128)(2,1)} custom-call(s32[64]{0:T(128)S(1)} %reshape.39.pair_ref, bf16[8,16,2,16,128]{4,3,2,1,0:T(8,128)(2,1)S(1)} %all-to-all-done.own_ref, bf16[8,16,2,16,128]{4,3,2,1,0:T(8,128)(2,1)S(1)} %all-to-all-done.1.far_ref, bf16[2,16,31,16,256]{4,3,2,1,0:T(8,128)(2,1)} %expand.2.low_ref, ...), custom_call_target="tpu_custom_call" | custom-call | tf_op jit(solution)/shard_map/translate/pallas_call | solution.py:319
  62.9 3.6 %all-to-all-start.3 = ((bf16[8,16,2,16,128]{4,3,2,1,0:T(8,128)(2,1)}), bf16[8,16,2,16,128]{4,3,2,1,0:T(8,128)(2,1)S(1)}, u32[]{:S(2)}, u32[]{:S(2)}) async-start(bf16[8,16,2,16,128]{4,3,2,1,0:T(8,128)(2,1)} %translate.3), calls=%async_computation.3 | async-start | bytes 2097152 | tf_op jit(solution)/shard_map/all_to_all | solution.py:223
  66.4 9.0 %translate.2 = bf16[8,16,2,16,128]{4,3,2,1,0:T(8,128)(2,1)} custom-call(s32[64]{0:T(128)S(1)} %reshape.39.pair_ref, bf16[8,16,2,16,128]{4,3,2,1,0:T(8,128)(2,1)S(1)} %all-to-all-done.own_ref, bf16[8,16,2,16,128]{4,3,2,1,0:T(8,128)(2,1)S(1)} %all-to-all-done.1.far_ref, bf16[2,16,31,16,256]{4,3,2,1,0:T(8,128)(2,1)} %expand.2.low_ref, ...), custom_call_target="tpu_custom_call" | custom-call | tf_op jit(solution)/shard_map/translate/pallas_call | solution.py:319
  75.4 5.4 %all-to-all-done.3 = bf16[8,16,2,16,128]{4,3,2,1,0:T(8,128)(2,1)S(1)} async-done(((bf16[8,16,2,16,128]{4,3,2,1,0:T(8,128)(2,1)}), bf16[8,16,2,16,128]{4,3,2,1,0:T(8,128)(2,1)S(1)}, u32[]{:S(2)}, u32[]{:S(2)}) %all-to-all-start.3) | async-done | bytes 1048608 | tf_op jit(solution)/shard_map/all_to_all | solution.py:223
  80.8 3.6 %all-to-all-start.2 = ((bf16[8,16,2,16,128]{4,3,2,1,0:T(8,128)(2,1)}), bf16[8,16,2,16,128]{4,3,2,1,0:T(8,128)(2,1)S(1)}, u32[]{:S(2)}, u32[]{:S(2)}) async-start(bf16[8,16,2,16,128]{4,3,2,1,0:T(8,128)(2,1)} %translate.2), calls=%async_computation.2 | async-start | bytes 2097152 | tf_op jit(solution)/shard_map/all_to_all | solution.py:223
  84.4 1.0 field.3
  85.3 0.7 collective-permute-start.1
  86.1 22.3 %all-to-all-done.2 = bf16[8,16,2,16,128]{4,3,2,1,0:T(8,128)(2,1)S(1)} async-done(((bf16[8,16,2,16,128]{4,3,2,1,0:T(8,128)(2,1)}), bf16[8,16,2,16,128]{4,3,2,1,0:T(8,128)(2,1)S(1)}, u32[]{:S(2)}, u32[]{:S(2)}) %all-to-all-start.2) | async-done | bytes 1048608 | tf_op jit(solution)/shard_map/all_to_all | solution.py:223
  108.3 1.0 field.2
  109.4 2.5 %collective-permute-done.1 = bf16[2048,128]{1,0:T(8,128)(2,1)S(1)} collective-permute-done((bf16[2048,128]{1,0:T(8,128)(2,1)S(1)}, bf16[2048,128]{1,0:T(8,128)(2,1)S(1)}, u32[]{:S(2)}, u32[]{:S(2)}) %collective-permute-start.1) | collective-permute-done | bytes 524320 | tf_op jit(solution)/shard_map/ppermute | solution.py:228
  111.8 0.9 add_convert_fusion
  (15 shorter events, 0.3 us)
Async XLA Ops:
  0.0 28.9 %collective-permute-start = (bf16[2048,128]{1,0:T(8,128)(2,1)}, bf16[2048,128]{1,0:T(8,128)(2,1)S(1)}, u32[]{:S(2)}, u32[]{:S(2)}) collective-permute-start(bf16[2048,128]{1,0:T(8,128)(2,1)} %bitcast.16), channel_id=1, source_target_pairs={{0,8},{4,12},{8,0},{12,4},{1,9},{5,13},{9,1},{13,5},{2,10},{6,14},... | collective-permute-start | bytes 1572872 | tf_op jit(solution)/shard_map/ppermute | solution.py:228
  7.7 28.3 %all-to-all-start = ((bf16[8,16,2,16,128]{4,3,2,1,0:T(8,128)(2,1)}), bf16[8,16,2,16,128]{4,3,2,1,0:T(8,128)(2,1)S(1)}, u32[]{:S(2)}, u32[]{:S(2)}) async-start(bf16[8,16,2,16,128]{4,3,2,1,0:T(8,128)(2,1)} %bitcast.15), calls=%async_computation | async-start | bytes 2097152 | tf_op jit(solution)/shard_map/all_to_all | solution.py:223
  21.8 7.0 %copy-start.1 = (bf16[2,128,512]{2,1,0:T(8,128)(2,1)S(1)}, bf16[2,128,512]{2,1,0:T(8,128)(2,1)}, u32[]{:S(2)}) copy-start(bf16[2,128,512]{2,1,0:T(8,128)(2,1)} %dis_ref.1) | copy-start | bytes 786436
  21.8 7.1 %copy-start = (bf16[2,512,128]{2,1,0:T(8,128)(2,1)S(1)}, bf16[2,512,128]{2,1,0:T(8,128)(2,1)}, u32[]{:S(2)}) copy-start(bf16[2,512,128]{2,1,0:T(8,128)(2,1)} %agg_ref.3) | copy-start | bytes 786436
  21.8 17.7 %copy-start.2 = (s32[8,8]{1,0:T(8,128)S(1)}, s32[8,8]{1,0:T(8,128)}, u32[]{:S(2)}) copy-start(s32[8,8]{1,0:T(8,128)} %param.10) | copy-start | bytes 772
  21.8 17.7 %copy-start.3 = (s32[8,8]{1,0:T(8,128)S(1)}, s32[8,8]{1,0:T(8,128)}, u32[]{:S(2)}) copy-start(s32[8,8]{1,0:T(8,128)} %param.11) | copy-start | bytes 772
  36.0 17.9 %all-to-all-start.1 = ((bf16[8,16,2,16,128]{4,3,2,1,0:T(8,128)(2,1)}), bf16[8,16,2,16,128]{4,3,2,1,0:T(8,128)(2,1)S(1)}, u32[]{:S(2)}, u32[]{:S(2)}) async-start(bf16[8,16,2,16,128]{4,3,2,1,0:T(8,128)(2,1)} %bitcast.9), calls=%async_computation.1 | async-start | bytes 2097152 | tf_op jit(solution)/shard_map/all_to_all | solution.py:223
  62.9 17.9 %all-to-all-start.3 = ((bf16[8,16,2,16,128]{4,3,2,1,0:T(8,128)(2,1)}), bf16[8,16,2,16,128]{4,3,2,1,0:T(8,128)(2,1)S(1)}, u32[]{:S(2)}, u32[]{:S(2)}) async-start(bf16[8,16,2,16,128]{4,3,2,1,0:T(8,128)(2,1)} %translate.3), calls=%async_computation.3 | async-start | bytes 2097152 | tf_op jit(solution)/shard_map/all_to_all | solution.py:223
  80.8 27.5 %all-to-all-start.2 = ((bf16[8,16,2,16,128]{4,3,2,1,0:T(8,128)(2,1)}), bf16[8,16,2,16,128]{4,3,2,1,0:T(8,128)(2,1)S(1)}, u32[]{:S(2)}, u32[]{:S(2)}) async-start(bf16[8,16,2,16,128]{4,3,2,1,0:T(8,128)(2,1)} %translate.2), calls=%async_computation.2 | async-start | bytes 2097152 | tf_op jit(solution)/shard_map/all_to_all | solution.py:223
  85.3 26.5 %collective-permute-start.1 = (bf16[2048,128]{1,0:T(8,128)(2,1)S(1)}, bf16[2048,128]{1,0:T(8,128)(2,1)S(1)}, u32[]{:S(2)}, u32[]{:S(2)}) collective-permute-start(bf16[2048,128]{1,0:T(8,128)(2,1)S(1)} %field.3), channel_id=1, source_target_pairs={{0,8},{4,12},{8,0},{12,4},{1,9},{5,13},{9,1},{13,5},{2,10},{6,14},... | collective-permute-start | bytes 1572872 | tf_op jit(solution)/shard_map/ppermute | solution.py:228

commit v6 on v5

--- a/solution.py
+++ b/solution.py
@@ -77,14 +77,14 @@
         wide[pl.ds(x + 1, rows, stride=PITCH), :] = picked[:, LANES:]
     for k in range(batch):
         for v in range(2):
-            out_ref[v, k, middle] = jnp.zeros(out_ref.shape[3:], jnp.bfloat16)
+            out_ref[v, k, middle - 1] = jnp.zeros(out_ref.shape[3:], jnp.bfloat16)
         for t in range(translators):
             if abs(t - middle) < 2:
                 continue
             for q in range(2):
                 row = ((q * batch + k) * tall + t) * PITCH
                 for v in range(2):
-                    out_ref[v, k, t, :, q * LANES:(q + 1) * LANES] = wide[
+                    out_ref[v, k, t if t < middle else t - 2, :, q * LANES:(q + 1) * LANES] = wide[
                         row + v * depth:row + (v + 1) * depth
                     ].astype(jnp.bfloat16)
 
@@ -289,7 +289,7 @@
                     ),
                 ],
                 out_specs=pl.BlockSpec(
-                    (2, batch, count, columns, 2 * LANES), lambda k, base: (0, k, 0, 0, 0)
+                    (2, batch, count - 2, columns, 2 * LANES), lambda k, base: (0, k, 0, 0, 0)
                 ),
                 scratch_shapes=[
                     pltpu.VMEM((2 * LANES, x_half * LANES), jnp.bfloat16),
@@ -297,7 +297,7 @@
                     pltpu.VMEM((2 * batch * x_half * PITCH + SPARE, LANES), jnp.float32),
                 ],
             ),
-            out_shape=jax.ShapeDtypeStruct((2, half, count, columns, 2 * LANES), jnp.bfloat16),
+            out_shape=jax.ShapeDtypeStruct((2, half, count - 2, columns, 2 * LANES), jnp.bfloat16),
             compiler_params=pltpu.CompilerParams(vmem_limit_bytes=56 * MIB),
             cost_estimate=pl.CostEstimate(
                 flops=8 * 2 * 2 * half * x_half * 2 * LANES * x_half * LANES,
@@ -311,7 +311,8 @@
     across_source, first, pattern = lax.optimization_barrier((across_source, first, pattern))
     received = own, exchange(outgoing(across_source, 16))
     expanded = first, expand(1)
-    pairs = jnp.where(far_mask == 1, tile_map, middle).reshape(-1)
+    slots = jnp.where(tile_map < middle, tile_map, tile_map - 2)
+    pairs = jnp.where(far_mask == 1, slots, middle - 1).reshape(-1)
     steps = 4
     part = (near, steps) + block[2:]
 
@@ -325,10 +326,10 @@
                     pl.BlockSpec(part, lambda k, pairs: (0, k, 0, 0, 0)),
                     pl.BlockSpec(part, lambda k, pairs: (0, k, 0, 0, 0)),
                     pl.BlockSpec(
-                        (1, steps, count, columns, 2 * LANES), lambda k, pairs: (v, k, 0, 0, 0)
+                        (1, steps, count - 2, columns, 2 * LANES), lambda k, pairs: (v, k, 0, 0, 0)
                     ),
                     pl.BlockSpec(
-                        (1, steps, count, columns, 2 * LANES), lambda k, pairs: (v, k, 0, 0, 0)
+                        (1, steps, count - 2, columns, 2 * LANES), lambda k, pairs: (v, k, 0, 0, 0)
                     ),
                 ],
                 out_specs=pl.BlockSpec(part, lambda k, pairs: (0, k, 0, 0, 0)),

time: 114 us -> 114 us (level)
  local copies, waits for them, and re-layouts: 9.7 us -> 11.7 us
  Pallas kernels: 40 us -> 38.1 us
    unnamed x9 -> x13, local copies, waits for them, and re-layouts: 7.98 us -> 9.95 us
    pallas_call x2, Pallas kernels: 17.9 us -> 16.2 us  [translate(): pl.pallas_call(functools.partial(translate_kernel, wide, slab, sub, rows,...]
  transfers between devices with their start and end apart: 6 -> 6, of which waited for: 5 -> 5; matrix products, arithmetic and copies ran while one was open for 9% -> 9% of each run, Pallas kernels for 28% -> 27%
where the time goes in v6:
time: 114 us; the launch traced here: 113 us
  waiting for transfers between devices  42.1 us (37%)
  Pallas kernels  38.1 us (33%)
  starting transfers between devices  19.2 us (17%)
  local copies, waits for them, and re-layouts  11.7 us (10%)
  other arithmetic  1.67 us (1%)
    all_to_all x4, waiting for transfers between devices, exchange(): lax.all_to_all(values, OWNERS, split_axis=0, concat_axis=0, tiled=True, a...  39.7 us
    pallas_call x2, Pallas kernels, translate(): pl.pallas_call(functools.partial(translate_kernel, wide, slab, sub, rows,...  16.2 us
    all_to_all x4, starting transfers between devices, exchange(): lax.all_to_all(values, OWNERS, split_axis=0, concat_axis=0, tiled=True, a...  14.4 us
    pallas_call x2, Pallas kernels, expand(): pl.pallas_call(functools.partial(expand_kernel, middle), grid_spec=pltpu....  13.7 us
    unnamed x13, local copies, waits for them, and re-layouts  9.95 us
    pallas_call x2, Pallas kernels, outgoing(): pl.pallas_call(functools.partial(outgoing_kernel, boxes, illum, near, hal...  6.07 us
    ppermute x2, starting transfers between devices, cross(): lax.ppermute(values, 'wide', [(w, (w + wide // 2) % wide) for w in range(...  4.76 us
    ppermute x2, waiting for transfers between devices, cross(): lax.ppermute(values, 'wide', [(w, (w + wide // 2) % wide) for w in range(...  2.47 us
  transfers between devices with their start and end apart: 6, of which 5 were waited for; matrix products, arithmetic and copies ran while one was open for 9% of the time, Pallas kernels for 27%

profile of v6, /device:TPU:0, one launch (start us, length us, event | category | flops | bytes accessed | tf_op | source)
XLA Modules:
  0.0 112.9 jit_solution(2783742679782492673)
XLA Ops:
  0.0 4.0 %collective-permute-start = (bf16[2048,128]{1,0:T(8,128)(2,1)}, bf16[2048,128]{1,0:T(8,128)(2,1)S(1)}, u32[]{:S(2)}, u32[]{:S(2)}) collective-permute-start(bf16[2048,128]{1,0:T(8,128)(2,1)} %bitcast.16), channel_id=1, source_target_pairs={{0,8},{4,12},{8,0},{12,4},{1,9},{5,13},{9,1},{13,5},{2,10},{6,14},... | collective-permute-start | bytes 1572872 | tf_op jit(solution)/shard_map/ppermute | solution.py:228
  4.0 3.6 %outgoing.2 = bf16[4096,128]{1,0:T(8,128)(2,1)} custom-call(s32[1]{0:T(128)} %bitcast.place_ref, bf16[2048,128]{1,0:T(8,128)(2,1)} %bitcast.17, bf16[2,512,128]{2,1,0:T(8,128)(2,1)} %agg_ref.3), custom_call_target="tpu_custom_call" | custom-call | tf_op jit(solution)/shard_map/outgoing/pallas_call | solution.py:231
  7.7 3.8 %all-to-all-start = ((bf16[8,16,2,16,128]{4,3,2,1,0:T(8,128)(2,1)}), bf16[8,16,2,16,128]{4,3,2,1,0:T(8,128)(2,1)S(1)}, u32[]{:S(2)}, u32[]{:S(2)}) async-start(bf16[8,16,2,16,128]{4,3,2,1,0:T(8,128)(2,1)} %bitcast.15), calls=%async_computation | async-start | bytes 2097152 | tf_op jit(solution)/shard_map/all_to_all | solution.py:223
  11.4 0.7 fusion.2
  12.2 0.9 fusion.3
  13.2 8.0 %copy.11.table_ref = bf16[2,128,31,255]{3,2,1,0:T(8,128)(2,1)} copy(bf16[2,128,31,255]{1,0,3,2:T(2,128)(2,1)} %param.9) | data formatting | bytes 8094720 | tf_op args[2]
  21.8 6.9 %expand.2.low_ref = bf16[2,16,29,16,256]{4,3,2,1,0:T(8,128)(2,1)} custom-call(s32[1]{0:T(128)} %bitcast.3.base_ref, s32[32,128]{1,0:T(8,128)} %pad_add_fusion.2.index_ref, bf16[2,128,31,255]{3,2,1,0:T(8,128)(2,1)} %copy.11.table_ref), custom_call_target="tpu_custom_call" | custom-call | flops 17179869184 | bytes 65011712 | tf_op jit(solution)/shard_map/expand/pallas_call | solution.py:279
  28.9 2.4 %outgoing.3 = bf16[4096,128]{1,0:T(8,128)(2,1)} custom-call(s32[1]{0:T(128)} %bitcast.place_ref, bf16[2048,128]{1,0:T(8,128)(2,1)S(1)} %collective-permute-done.src_ref, bf16[2,512,128]{2,1,0:T(8,128)(2,1)S(1)} %copy-done.2), custom_call_target="tpu_custom_call" | custom-call | tf_op jit(solution)/shard_map/outgoing/pallas_call | solution.py:231
  31.3 4.6 %all-to-all-done.own_ref = bf16[8,16,2,16,128]{4,3,2,1,0:T(8,128)(2,1)S(1)} async-done(((bf16[8,16,2,16,128]{4,3,2,1,0:T(8,128)(2,1)}), bf16[8,16,2,16,128]{4,3,2,1,0:T(8,128)(2,1)S(1)}, u32[]{:S(2)}, u32[]{:S(2)}) %all-to-all-start) | async-done | bytes 1048608 | tf_op jit(solution)/shard_map/all_to_all | solution.py:223
  36.0 3.6 %all-to-all-start.1 = ((bf16[8,16,2,16,128]{4,3,2,1,0:T(8,128)(2,1)}), bf16[8,16,2,16,128]{4,3,2,1,0:T(8,128)(2,1)S(1)}, u32[]{:S(2)}, u32[]{:S(2)}) async-start(bf16[8,16,2,16,128]{4,3,2,1,0:T(8,128)(2,1)} %bitcast.9), calls=%async_computation.1 | async-start | bytes 2097152 | tf_op jit(solution)/shard_map/all_to_all | solution.py:223
  39.7 6.8 %expand.3.high_ref = bf16[2,16,29,16,256]{4,3,2,1,0:T(8,128)(2,1)} custom-call(s32[1]{0:T(128)} %bitcast.3.base_ref, s32[32,128]{1,0:T(8,128)} %pad_add_fusion.2.index_ref, bf16[2,128,31,255]{3,2,1,0:T(8,128)(2,1)} %copy.11.table_ref), custom_call_target="tpu_custom_call" | custom-call | flops 17179869184 | bytes 65011712 | tf_op jit(solution)/shard_map/expand/pallas_call | solution.py:279
  46.5 7.5 %all-to-all-done.1.far_ref = bf16[8,16,2,16,128]{4,3,2,1,0:T(8,128)(2,1)S(1)} async-done(((bf16[8,16,2,16,128]{4,3,2,1,0:T(8,128)(2,1)}), bf16[8,16,2,16,128]{4,3,2,1,0:T(8,128)(2,1)S(1)}, u32[]{:S(2)}, u32[]{:S(2)}) %all-to-all-start.1) | async-done | bytes 1048608 | tf_op jit(solution)/shard_map/all_to_all | solution.py:223
  53.9 8.1 %translate.3 = bf16[8,16,2,16,128]{4,3,2,1,0:T(8,128)(2,1)S(1)} custom-call(s32[64]{0:T(128)S(1)} %reshape.39.pair_ref, bf16[8,16,2,16,128]{4,3,2,1,0:T(8,128)(2,1)S(1)} %all-to-all-done.own_ref, bf16[8,16,2,16,128]{4,3,2,1,0:T(8,128)(2,1)S(1)} %all-to-all-done.1.far_ref, bf16[2,16,29,16,256]{4,3,2,1,0:T(8,128)(2,1)} %expand.2.low_ref, ...), custom_call_target="tpu_custom_call" | custom-call | tf_op jit(solution)/shard_map/translate/pallas_call | solution.py:320
  62.0 1.0 copy-done.1
  63.0 3.6 %all-to-all-start.3 = ((bf16[8,16,2,16,128]{4,3,2,1,0:T(8,128)(2,1)}), bf16[8,16,2,16,128]{4,3,2,1,0:T(8,128)(2,1)S(1)}, u32[]{:S(2)}, u32[]{:S(2)}) async-start(bf16[8,16,2,16,128]{4,3,2,1,0:T(8,128)(2,1)} %copy-done.1), calls=%async_computation.3 | async-start | bytes 2097152 | tf_op jit(solution)/shard_map/all_to_all | solution.py:223
  66.6 8.1 %translate.2 = bf16[8,16,2,16,128]{4,3,2,1,0:T(8,128)(2,1)S(1)} custom-call(s32[64]{0:T(128)S(1)} %reshape.39.pair_ref, bf16[8,16,2,16,128]{4,3,2,1,0:T(8,128)(2,1)S(1)} %all-to-all-done.own_ref, bf16[8,16,2,16,128]{4,3,2,1,0:T(8,128)(2,1)S(1)} %all-to-all-done.1.far_ref, bf16[2,16,29,16,256]{4,3,2,1,0:T(8,128)(2,1)} %expand.2.low_ref, ...), custom_call_target="tpu_custom_call" | custom-call | tf_op jit(solution)/shard_map/translate/pallas_call | solution.py:320
  74.7 1.0 copy-done
  75.7 5.3 %all-to-all-done.3 = bf16[8,16,2,16,128]{4,3,2,1,0:T(8,128)(2,1)S(1)} async-done(((bf16[8,16,2,16,128]{4,3,2,1,0:T(8,128)(2,1)}), bf16[8,16,2,16,128]{4,3,2,1,0:T(8,128)(2,1)S(1)}, u32[]{:S(2)}, u32[]{:S(2)}) %all-to-all-start.3) | async-done | bytes 1048608 | tf_op jit(solution)/shard_map/all_to_all | solution.py:223
  81.0 3.6 %all-to-all-start.2 = ((bf16[8,16,2,16,128]{4,3,2,1,0:T(8,128)(2,1)}), bf16[8,16,2,16,128]{4,3,2,1,0:T(8,128)(2,1)S(1)}, u32[]{:S(2)}, u32[]{:S(2)}) async-start(bf16[8,16,2,16,128]{4,3,2,1,0:T(8,128)(2,1)} %copy-done), calls=%async_computation.2 | async-start | bytes 2097152 | tf_op jit(solution)/shard_map/all_to_all | solution.py:223
  84.5 1.0 field.3
  86.2 22.3 %all-to-all-done.2 = bf16[8,16,2,16,128]{4,3,2,1,0:T(8,128)(2,1)S(1)} async-done(((bf16[8,16,2,16,128]{4,3,2,1,0:T(8,128)(2,1)}), bf16[8,16,2,16,128]{4,3,2,1,0:T(8,128)(2,1)S(1)}, u32[]{:S(2)}, u32[]{:S(2)}) %all-to-all-start.2) | async-done | bytes 1048608 | tf_op jit(solution)/shard_map/all_to_all | solution.py:223
  108.5 1.0 field.2
  109.5 2.5 %collective-permute-done.1 = bf16[2048,128]{1,0:T(8,128)(2,1)S(1)} collective-permute-done((bf16[2048,128]{1,0:T(8,128)(2,1)S(1)}, bf16[2048,128]{1,0:T(8,128)(2,1)S(1)}, u32[]{:S(2)}, u32[]{:S(2)}) %collective-permute-start.1) | collective-permute-done | bytes 524320 | tf_op jit(solution)/shard_map/ppermute | solution.py:228
  112.0 0.9 add_convert_fusion
  (19 shorter events, 1.7 us)
Async XLA Ops:
  0.0 28.9 %collective-permute-start = (bf16[2048,128]{1,0:T(8,128)(2,1)}, bf16[2048,128]{1,0:T(8,128)(2,1)S(1)}, u32[]{:S(2)}, u32[]{:S(2)}) collective-permute-start(bf16[2048,128]{1,0:T(8,128)(2,1)} %bitcast.16), channel_id=1, source_target_pairs={{0,8},{4,12},{8,0},{12,4},{1,9},{5,13},{9,1},{13,5},{2,10},{6,14},... | collective-permute-start | bytes 1572872 | tf_op jit(solution)/shard_map/ppermute | solution.py:228
  7.7 28.3 %all-to-all-start = ((bf16[8,16,2,16,128]{4,3,2,1,0:T(8,128)(2,1)}), bf16[8,16,2,16,128]{4,3,2,1,0:T(8,128)(2,1)S(1)}, u32[]{:S(2)}, u32[]{:S(2)}) async-start(bf16[8,16,2,16,128]{4,3,2,1,0:T(8,128)(2,1)} %bitcast.15), calls=%async_computation | async-start | bytes 2097152 | tf_op jit(solution)/shard_map/all_to_all | solution.py:223
  21.8 6.9 %copy-start.3 = (bf16[2,128,512]{2,1,0:T(8,128)(2,1)S(1)}, bf16[2,128,512]{2,1,0:T(8,128)(2,1)}, u32[]{:S(2)}) copy-start(bf16[2,128,512]{2,1,0:T(8,128)(2,1)} %dis_ref.1) | copy-start | bytes 786436
  21.8 7.1 %copy-start.2 = (bf16[2,512,128]{2,1,0:T(8,128)(2,1)S(1)}, bf16[2,512,128]{2,1,0:T(8,128)(2,1)}, u32[]{:S(2)}) copy-start(bf16[2,512,128]{2,1,0:T(8,128)(2,1)} %agg_ref.3) | copy-start | bytes 786436
  21.8 17.7 %copy-start.4 = (s32[8,8]{1,0:T(8,128)S(1)}, s32[8,8]{1,0:T(8,128)}, u32[]{:S(2)}) copy-start(s32[8,8]{1,0:T(8,128)} %param.10) | copy-start | bytes 772
  21.8 17.7 %copy-start.5 = (s32[8,8]{1,0:T(8,128)S(1)}, s32[8,8]{1,0:T(8,128)}, u32[]{:S(2)}) copy-start(s32[8,8]{1,0:T(8,128)} %param.11) | copy-start | bytes 772
  36.0 17.9 %all-to-all-start.1 = ((bf16[8,16,2,16,128]{4,3,2,1,0:T(8,128)(2,1)}), bf16[8,16,2,16,128]{4,3,2,1,0:T(8,128)(2,1)S(1)}, u32[]{:S(2)}, u32[]{:S(2)}) async-start(bf16[8,16,2,16,128]{4,3,2,1,0:T(8,128)(2,1)} %bitcast.9), calls=%async_computation.1 | async-start | bytes 2097152 | tf_op jit(solution)/shard_map/all_to_all | solution.py:223
  62.0 1.0 copy-start.1
  63.0 17.9 %all-to-all-start.3 = ((bf16[8,16,2,16,128]{4,3,2,1,0:T(8,128)(2,1)}), bf16[8,16,2,16,128]{4,3,2,1,0:T(8,128)(2,1)S(1)}, u32[]{:S(2)}, u32[]{:S(2)}) async-start(bf16[8,16,2,16,128]{4,3,2,1,0:T(8,128)(2,1)} %copy-done.1), calls=%async_computation.3 | async-start | bytes 2097152 | tf_op jit(solution)/shard_map/all_to_all | solution.py:223
  74.7 1.0 copy-start
  81.0 27.5 %all-to-all-start.2 = ((bf16[8,16,2,16,128]{4,3,2,1,0:T(8,128)(2,1)}), bf16[8,16,2,16,128]{4,3,2,1,0:T(8,128)(2,1)S(1)}, u32[]{:S(2)}, u32[]{:S(2)}) async-start(bf16[8,16,2,16,128]{4,3,2,1,0:T(8,128)(2,1)} %copy-done), calls=%async_computation.2 | async-start | bytes 2097152 | tf_op jit(solution)/shard_map/all_to_all | solution.py:223
  85.5 26.5 %collective-permute-start.1 = (bf16[2048,128]{1,0:T(8,128)(2,1)S(1)}, bf16[2048,128]{1,0:T(8,128)(2,1)S(1)}, u32[]{:S(2)}, u32[]{:S(2)}) collective-permute-start(bf16[2048,128]{1,0:T(8,128)(2,1)S(1)} %field.3), channel_id=1, source_target_pairs={{0,8},{4,12},{8,0},{12,4},{1,9},{5,13},{9,1},{13,5},{2,10},{6,14},... | collective-permute-start | bytes 1572872 | tf_op jit(solution)/shard_map/ppermute | solution.py:228
